TPU v7x, 128 devices: a whole 4x4x4 slice. The times are simulated.
128 devices in a mesh: section: 2 (over y_hi), dp: 16 (over x, y_lo, core), tensor: 4 (over z).
Axes of the slice: x: 4, y: 4 (y_hi: 2, y_lo: 2; y = y_hi * 2 + y_lo), z: 4, core: 2. Of those that a mesh axis runs over, the one named last changes fastest.
Arguments:
- inputs: bfloat16 [2, 4096, 1024], P(None, ('dp', 'tensor')), may hold values from -6 to 6
- cotangent: bfloat16 [2, 4096, 1024], P(None, ('dp', 'tensor')), may hold values from -6 to 6
- segments: int32 [2, 16, 256], P(None, 'dp'), may hold values from 0 to 3, as said below
- qkv_weight: bfloat16 [2, 1024, 3, 1024], P('section', 'dp', None, 'tensor'), may hold values from -0.25 to 0.25
- out_weight: bfloat16 [2, 1024, 1024], P('section', 'tensor', 'dp'), may hold values from -0.5 to 0.5
- fc1_weight: bfloat16 [2, 1024, 4096], P('section', 'dp', 'tensor'), may hold values from -0.1875 to 0.1875
- fc2_weight: bfloat16 [2, 4096, 1024], P('section', 'tensor', 'dp'), may hold values from -0.09375 to 0.09375
- ln_gains: float32 [2, 2, 1024], P('section'), may hold values from 0.25 to 1.75
- ln_biases: float32 [2, 2, 1024], P('section'), may hold values from -2.5 to 2.5
- qv_bias: float32 [2, 2, 1024], P('section'), may hold values from -2.5 to 2.5
- proj_biases: float32 [2, 2, 1024], P('section'), may hold values from -2.5 to 2.5
- fc_bias: float32 [2, 4096], P('section'), may hold values from -2.5 to 2.5
Outputs:
- section_outputs: float32 [2, 2, 4096, 1024], P('section', None, ('dp', 'tensor'))
- section_grads: float32 [2, 2, 4096, 1024], P('section', None, ('dp', 'tensor'))
- qkv_grad: float32 [2, 1024, 3, 1024], P('section', 'dp', None, 'tensor')
- out_grad: float32 [2, 1024, 1024], P('section', 'tensor', 'dp')
- fc1_grad: float32 [2, 1024, 4096], P('section', 'dp', 'tensor')
- fc2_grad: float32 [2, 4096, 1024], P('section', 'tensor', 'dp')
- gain_grad: float32 [2, 2, 1024], P('section')
- offset_grad: float32 [2, 2, 1024], P('section')
- qv_bias_grad: float32 [2, 2, 1024], P('section')
- proj_bias_grad: float32 [2, 2, 1024], P('section')
- fc_bias_grad: float32 [2, 4096], P('section')
Inputs may be any that keep to these rules, and one draw needn't show every extreme that they name: `segments`: in every row of 256 tokens the ids run 0, 1, 2, 3 in order, never falling, each present; document 1 starts within the row's first 64 tokens and ends within its last 64 tokens.
All inputs are finite; a program needn't handle non-finite values.
Results may differ from a plain program's by a relative error of at most 0.02.
Values may be sent and summed in bfloat16 or wider, within the bound.
A program may use at most 128 MiB of HBM per device.

v0:
```python
import math

import jax
import jax.numpy as jnp
from jax import lax
from jax.sharding import PartitionSpec as P

D = 1024
HD = 64
FF = 4096


NEGATIVE = -1000000000.0
GELU_COEF = 0.7978845608028654
EPSILON = 1e-05


def passed_along(value, axis, steps):
    count = lax.axis_size(axis)
    first, last = (max(0, -steps), min(count, count - steps))
    return lax.ppermute(value, axis, [(source, source + steps) for source in range(first, last)])


def dot_plain(left_side, right_side):
    return jnp.dot(left_side, right_side, preferred_element_type=jnp.float32)


def dot_rows(left_side, right_side):
    return lax.dot_general(
        left_side, right_side, (((0,), (0,)), ((), ())), preferred_element_type=jnp.float32
    )


def dot_cols(left_side, right_side):
    return lax.dot_general(
        left_side, right_side, (((1,), (1,)), ((), ())), preferred_element_type=jnp.float32
    )


def norm_rows(hidden, gain_row, offset_row):
    centre = hidden - jnp.mean(hidden, axis=-1, keepdims=True)
    spread = jnp.mean(centre * centre, axis=-1, keepdims=True)
    inverse = lax.rsqrt(spread + EPSILON)
    unit_rows = centre * inverse
    return (unit_rows * gain_row + offset_row, unit_rows, inverse)


def norm_back(grad_rows, unit_rows, inverse, gain_row):
    grad_unit = grad_rows * gain_row
    grad_hidden = inverse * (
        grad_unit
        - jnp.mean(grad_unit, axis=-1, keepdims=True)
        - unit_rows * jnp.mean(grad_unit * unit_rows, axis=-1, keepdims=True)
    )
    return (grad_hidden, jnp.sum(grad_rows * unit_rows, axis=0), jnp.sum(grad_rows, axis=0))


def gelu_both(before):
    cubic_part = before + 0.044715 * before * before * before
    tanh_part = jnp.tanh(GELU_COEF * cubic_part)
    value_out = 0.5 * before * (1.0 + tanh_part)
    slopes = 0.5 * (1.0 + tanh_part) + 0.5 * before * (1.0 - tanh_part * tanh_part) * GELU_COEF * (
        1.0 + 3.0 * 0.044715 * before * before
    )
    return (value_out, slopes)


def block_scores(query_block, key_heads, seg_row, block_start, block_rows):
    scale_factor = 1.0 / math.sqrt(HD)
    scores = (
        jnp.einsum("qhd,khd->hqk", query_block, key_heads, preferred_element_type=jnp.float32)
        * scale_factor
    )
    query_places = block_start + jnp.arange(block_rows)
    key_places = jnp.arange(seg_row.shape[0])
    allowed = (seg_row[:, None] == seg_row[None, :]) & (
        query_places[:, None] >= key_places[None, :]
    )
    return jnp.where(allowed[None], scores, NEGATIVE)


def attend_forward(queries, key_rows, value_rows, seg_row):
    seq_len = queries.shape[0]
    heads_here = queries.shape[1] // HD
    block_rows = min(512, seq_len)
    query_heads = queries.reshape(seq_len, heads_here, HD)
    key_heads = key_rows.reshape(seq_len, heads_here, HD)
    value_heads = value_rows.reshape(seq_len, heads_here, HD)

    def one_block(block_start):
        scores = block_scores(query_heads, key_heads, seg_row, block_start, block_rows)
        row_max = jnp.max(scores, axis=-1, keepdims=True)
        shifted = jnp.exp(scores - row_max)
        row_total = jnp.sum(shifted, axis=-1, keepdims=True)
        attn_probs = shifted / row_total
        mixed_block = jnp.einsum(
            "hqk,khd->qhd",
            attn_probs.astype(jnp.bfloat16),
            value_heads,
            preferred_element_type=jnp.float32,
        )
        return (
            mixed_block.reshape(block_rows, heads_here * HD).astype(jnp.bfloat16),
            (row_max + jnp.log(row_total))[:, :, 0],
        )

    starts = jnp.arange(seq_len // block_rows) * block_rows
    mixed_blocks, log_blocks = lax.map(one_block, starts)
    mixed_rows = mixed_blocks.reshape(seq_len, heads_here * HD)
    log_total = jnp.transpose(log_blocks, (1, 0, 2)).reshape(heads_here, seq_len)
    return (mixed_rows, log_total)


def attend_back(queries, key_rows, value_rows, log_total, grad_mixed, seg_row):
    seq_len = queries.shape[0]
    heads_here = queries.shape[1] // HD
    block_rows = min(512, seq_len)
    scale_factor = 1.0 / math.sqrt(HD)
    query_heads = queries.reshape(seq_len, heads_here, HD)
    key_heads = key_rows.reshape(seq_len, heads_here, HD)
    value_heads = value_rows.reshape(seq_len, heads_here, HD)
    grad_heads = grad_mixed.reshape(seq_len, heads_here, HD)

    def one_block(carried, block_start):
        key_acc, value_acc = carried
        scores = block_scores(query_heads, key_heads, seg_row, block_start, block_rows)
        attn_probs = jnp.exp(scores - log_total[:, :, None])
        grad_probs = jnp.einsum(
            "qhd,khd->hqk", grad_heads, value_heads, preferred_element_type=jnp.float32
        )
        row_dot = jnp.sum(attn_probs * grad_probs, axis=-1, keepdims=True)
        grad_scores = (attn_probs * (grad_probs - row_dot)).astype(jnp.bfloat16)
        grad_query = (
            jnp.einsum("hqk,khd->qhd", grad_scores, key_heads, preferred_element_type=jnp.float32)
            * scale_factor
        )
        key_acc = (
            key_acc
            + jnp.einsum(
                "hqk,qhd->khd", grad_scores, query_heads, preferred_element_type=jnp.float32
            )
            * scale_factor
        )
        value_acc = value_acc + jnp.einsum(
            "hqk,qhd->khd",
            attn_probs.astype(jnp.bfloat16),
            grad_heads,
            preferred_element_type=jnp.float32,
        )
        return ((key_acc, value_acc), grad_query)

    zero_heads = jnp.zeros((seq_len, heads_here, HD), jnp.float32)
    starts = jnp.arange(seq_len // block_rows) * block_rows
    (key_grad, value_grad), query_grad = lax.scan(one_block, (zero_heads, zero_heads), starts)
    local_width = heads_here * HD
    return (
        query_grad.reshape(seq_len, local_width),
        key_grad.reshape(seq_len, local_width),
        value_grad.reshape(seq_len, local_width),
    )


def local(
    inputs,
    cotangent,
    segments,
    qkv_weight,
    out_weight,
    fc1_weight,
    fc2_weight,
    ln_gains,
    ln_biases,
    qv_bias,
    proj_biases,
    fc_bias,
):
    micro_count = inputs.shape[0]
    rows_local = inputs.shape[1]
    section_index = lax.axis_index("section")
    tensor_index = lax.axis_index("tensor")
    local_cols = qkv_weight.shape[3]
    hidden_local = fc1_weight.shape[2]
    qkv_full, out_full, fc1_full, fc2_full = (
        lax.all_gather(qkv_weight[0], "dp", axis=0, tiled=True),
        lax.all_gather(out_weight[0], "dp", axis=1, tiled=True),
        lax.all_gather(fc1_weight[0], "dp", axis=0, tiled=True),
        lax.all_gather(fc2_weight[0], "dp", axis=1, tiled=True),
    )
    qkv_flat = qkv_full.reshape(D, 3 * local_cols)
    gain_rows = ln_gains[0]
    offset_rows = ln_biases[0]
    proj_rows = proj_biases[0]
    qv_local = lax.dynamic_slice_in_dim(qv_bias[0], tensor_index * local_cols, local_cols, 1)
    fc_local = lax.dynamic_slice_in_dim(fc_bias[0], tensor_index * hidden_local, hidden_local, 0)
    seg_rows = segments[:, 0]
    pass_rows = jnp.zeros((rows_local, D), jnp.bfloat16)
    saved_ticks = []
    out_ticks = []
    for tick_step in range(micro_count + 1):
        batch_index = jnp.clip(tick_step - section_index, 0, micro_count - 1)
        own_rows = lax.dynamic_index_in_dim(inputs, batch_index, 0, keepdims=False)
        layer_in = jnp.where(section_index == 0, own_rows, pass_rows).astype(jnp.float32)
        seg_row = lax.dynamic_index_in_dim(seg_rows, batch_index, 0, keepdims=False)
        normed_one, forward_unit_one, forward_inverse_one = norm_rows(
            layer_in, gain_rows[0], offset_rows[0]
        )
        forward_gathered_one = lax.all_gather(
            normed_one.astype(jnp.bfloat16), "tensor", axis=0, tiled=True
        )
        forward_seq_len = forward_gathered_one.shape[0]
        projected = dot_plain(forward_gathered_one, qkv_flat).reshape(
            forward_seq_len, 3, local_cols
        )
        forward_queries = (projected[:, 0] + qv_local[0]).astype(jnp.bfloat16)
        forward_key_rows = projected[:, 1].astype(jnp.bfloat16)
        forward_value_rows = (projected[:, 2] + qv_local[1]).astype(jnp.bfloat16)
        forward_mixed_rows, forward_log_total = attend_forward(
            forward_queries, forward_key_rows, forward_value_rows, seg_row
        )
        attn_rows = lax.psum_scatter(
            dot_plain(forward_mixed_rows, out_full), "tensor", scatter_dimension=0, tiled=True
        )
        middle = layer_in + (attn_rows + proj_rows[0])
        normed_two, forward_unit_two, forward_inverse_two = norm_rows(
            middle, gain_rows[1], offset_rows[1]
        )
        forward_gathered_two = lax.all_gather(
            normed_two.astype(jnp.bfloat16), "tensor", axis=0, tiled=True
        )
        active, forward_slopes = gelu_both(dot_plain(forward_gathered_two, fc1_full) + fc_local)
        forward_active_low = active.astype(jnp.bfloat16)
        mlp_rows = lax.psum_scatter(
            dot_plain(forward_active_low, fc2_full), "tensor", scatter_dimension=0, tiled=True
        )
        layer_out = middle + (mlp_rows + proj_rows[1])
        layer_out, saved_state = (
            layer_out,
            (
                forward_unit_one,
                forward_inverse_one,
                forward_gathered_one,
                forward_queries,
                forward_key_rows,
                forward_value_rows,
                forward_log_total,
                forward_mixed_rows,
                forward_unit_two,
                forward_inverse_two,
                forward_gathered_two,
                forward_slopes,
                forward_active_low,
            ),
        )
        if tick_step < micro_count:
            pass_rows = passed_along(layer_out.astype(jnp.bfloat16), "section", 1)
        saved_ticks.append(saved_state + (seg_row,))
        out_ticks.append(layer_out)
    section_out = lax.dynamic_slice_in_dim(jnp.stack(out_ticks), section_index, micro_count, 0)
    saved_all = jax.tree.map(lambda *leaves: jnp.stack(leaves), *saved_ticks)
    pass_grad = jnp.zeros((rows_local, D), jnp.bfloat16)
    grad_ticks = []
    weight_sums = None
    small_sums = None
    for tick_step in range(micro_count + 1):
        batch_raw = tick_step - 1 + section_index
        is_valid = ((batch_raw >= 0) & (batch_raw < micro_count)).astype(jnp.float32)
        batch_index = jnp.clip(batch_raw, 0, micro_count - 1)
        own_grad = lax.dynamic_index_in_dim(cotangent, batch_index, 0, keepdims=False)
        grad_out = jnp.where(section_index == 1, own_grad, pass_grad).astype(jnp.float32)
        saved_state = jax.tree.map(
            lambda member: lax.dynamic_index_in_dim(
                member, batch_index + section_index, 0, keepdims=False
            ),
            saved_all,
        )
        (
            unit_one,
            inverse_one,
            gathered_one,
            queries,
            key_rows,
            value_rows,
            log_total,
            mixed_rows,
            unit_two,
            inverse_two,
            gathered_two,
            slopes,
            active_low,
            backward_seg_row,
        ) = saved_state
        grad_mlp = lax.all_gather(grad_out.astype(jnp.bfloat16), "tensor", axis=0, tiled=True)
        fc2_grad = dot_rows(active_low, grad_mlp)
        grad_before = dot_cols(grad_mlp, fc2_full) * slopes
        grad_before_low = grad_before.astype(jnp.bfloat16)
        fc1_grad = dot_rows(gathered_two, grad_before_low)
        grad_normed_two = lax.psum_scatter(
            dot_cols(grad_before_low, fc1_full), "tensor", scatter_dimension=0, tiled=True
        )
        grad_norm_two, gain_two, offset_two = norm_back(
            grad_normed_two, unit_two, inverse_two, gain_rows[1]
        )
        grad_middle = grad_out + grad_norm_two
        grad_attn = lax.all_gather(grad_middle.astype(jnp.bfloat16), "tensor", axis=0, tiled=True)
        out_grad = dot_rows(mixed_rows, grad_attn)
        grad_mixed = dot_cols(grad_attn, out_full).astype(jnp.bfloat16)
        grad_queries, grad_keys, grad_values = attend_back(
            queries, key_rows, value_rows, log_total, grad_mixed, backward_seg_row
        )
        seq_len = grad_queries.shape[0]
        grad_proj = (
            jnp.stack([grad_queries, grad_keys, grad_values], axis=1)
            .astype(jnp.bfloat16)
            .reshape(seq_len, 3 * local_cols)
        )
        qkv_grad = dot_rows(gathered_one, grad_proj).reshape(D, 3, local_cols)
        grad_normed_one = lax.psum_scatter(
            dot_cols(grad_proj, qkv_flat), "tensor", scatter_dimension=0, tiled=True
        )
        grad_norm_one, gain_one, offset_one = norm_back(
            grad_normed_one, unit_one, inverse_one, gain_rows[0]
        )
        grad_in = grad_middle + grad_norm_one
        qv_terms = jnp.stack([jnp.sum(grad_queries, axis=0), jnp.sum(grad_values, axis=0)])
        qv_padded = lax.dynamic_update_slice_in_dim(
            jnp.zeros((2, D), jnp.float32), qv_terms, tensor_index * local_cols, 1
        )
        fc_padded = lax.dynamic_update_slice_in_dim(
            jnp.zeros((FF,), jnp.float32),
            jnp.sum(grad_before, axis=0),
            tensor_index * hidden_local,
            0,
        )
        small_terms = (
            jnp.stack([gain_one, gain_two]),
            jnp.stack([offset_one, offset_two]),
            jnp.stack([jnp.sum(grad_middle, axis=0), jnp.sum(grad_out, axis=0)]),
            qv_padded,
            fc_padded,
        )
        grad_in, weight_terms, small_terms = (
            grad_in,
            (qkv_grad, out_grad, fc1_grad, fc2_grad),
            small_terms,
        )
        weight_terms = jax.tree.map(lambda member: member * is_valid, weight_terms)
        small_terms = jax.tree.map(lambda member: member * is_valid, small_terms)
        weight_sums = (
            weight_terms
            if weight_sums is None
            else jax.tree.map(jnp.add, weight_sums, weight_terms)
        )
        small_sums = (
            small_terms if small_sums is None else jax.tree.map(jnp.add, small_sums, small_terms)
        )
        if tick_step < micro_count:
            pass_grad = passed_along(grad_in.astype(jnp.bfloat16), "section", -1)
        grad_ticks.append(grad_in)
    weight_sums = (
        lax.psum_scatter(weight_sums[0], "dp", scatter_dimension=0, tiled=True),
        lax.psum_scatter(weight_sums[1], "dp", scatter_dimension=1, tiled=True),
        lax.psum_scatter(weight_sums[2], "dp", scatter_dimension=0, tiled=True),
        lax.psum_scatter(weight_sums[3], "dp", scatter_dimension=1, tiled=True),
    )
    section_grad = lax.dynamic_slice_in_dim(
        jnp.stack(grad_ticks), 1 - section_index, micro_count, 0
    )
    gain_grad, offset_grad, proj_grad, qv_grad, fc_grad = lax.psum(
        (small_sums[0], small_sums[1], small_sums[2], small_sums[3], small_sums[4]),
        ("dp", "tensor"),
    )
    return (
        section_out[None],
        section_grad[None],
        weight_sums[0][None],
        weight_sums[1][None],
        weight_sums[2][None],
        weight_sums[3][None],
        gain_grad[None],
        offset_grad[None],
        qv_grad[None],
        proj_grad[None],
        fc_grad[None],
    )


def solution(mesh):
    in_specs = (
        P(None, ("dp", "tensor"), None),
        P(None, ("dp", "tensor"), None),
        P(None, "dp", None),
        P("section", "dp", None, "tensor"),
        P("section", "tensor", "dp"),
        P("section", "dp", "tensor"),
        P("section", "tensor", "dp"),
        P("section", None, None),
        P("section", None, None),
        P("section", None, None),
        P("section", None, None),
        P("section", None),
    )
    out_specs = (
        P("section", None, ("dp", "tensor"), None),
        P("section", None, ("dp", "tensor"), None),
        P("section", "dp", None, "tensor"),
        P("section", "tensor", "dp"),
        P("section", "dp", "tensor"),
        P("section", "tensor", "dp"),
        P("section", None, None),
        P("section", None, None),
        P("section", None, None),
        P("section", None, None),
        P("section", None),
    )
    return jax.shard_map(local, mesh=mesh, in_specs=in_specs, out_specs=out_specs, check_vma=False)
```

profile of v0, /device:TPU:0, one launch (start us, length us, event | category | flops | bytes accessed | tf_op | source)
XLA Modules:
  0.0 942.9 jit_solution(11150964306754761243)
XLA Ops:
  17.4 14.1 %all_gather.48 = bf16[256,1024]{1,0:T(8,128)(2,1)S(1)} all-gather(bf16[64,1024]{1,0:T(8,128)(2,1)S(1)} %fusion.172), channel_id=1, replica_groups=mesh['section'=2,'dp'=16,'tensor'=4] {'tensor'}, dimensions={0}, use_global_device_ids=true | all-gather | bytes 655360 | tf_op jit(solution)/shard_map/all_gather | solution.py:207
  31.6 21.4 %all-gather.1 = bf16[1,256,1024]{1,2,0:T(8,128)(2,1)S(1)} all-gather(bf16[1,256,64]{1,2,0:T(8,128)(2,1)} %param.16), channel_id=3, replica_groups=mesh['section'=2,'dp'=16,'tensor'=4] {'dp'}, dimensions={2}, use_global_device_ids=true | all-gather | bytes 557056 | tf_op jit(solution)/shard_map/all_gather | solution.py:185
  59.4 21.5 %reduce-scatter.19.cloned.1.call-done = f32[64,1024]{1,0:T(8,128)} async-done(((f32[256,1024]{1,0:T(8,128)}), f32[64,1024]{1,0:T(8,128)}) %reduce-scatter.19.cloned.1.call-update) | async-done | bytes 262160 | tf_op jit(solution)/shard_map/reduce_scatter | solution.py:220
  83.7 13.9 %all_gather.51 = bf16[256,1024]{1,0:T(8,128)(2,1)} all-gather(bf16[64,1024]{1,0:T(8,128)(2,1)S(1)} %get-tuple-element.288), channel_id=1, replica_groups=mesh['section'=2,'dp'=16,'tensor'=4] {'tensor'}, dimensions={0}, use_global_device_ids=true | all-gather | bytes 655360 | tf_op jit(solution)/shard_map/all_gather | solution.py:227
  97.6 18.7 %all-gather.11.cloned.1.call-done = bf16[1,1024,1024]{2,1,0:T(8,128)(2,1)} async-done(((bf16[1,64,1024]{2,1,0:T(8,128)(2,1)}), bf16[1,1024,1024]{2,1,0:T(8,128)(2,1)}) %all-gather.11.cloned.1.call-update) | async-done | bytes 2097168 | tf_op jit(solution)/shard_map/all_gather | solution.py:186
  119.7 32.4 %all-gather.13.cloned.1.call-done = bf16[1,1024,1024]{1,2,0:T(8,128)(2,1)} async-done(((bf16[1,1024,64]{1,2,0:T(8,128)(2,1)}), bf16[1,1024,1024]{1,2,0:T(8,128)(2,1)}) %all-gather.13.cloned.1.call-update) | async-done | bytes 2097168 | tf_op jit(solution)/shard_map/all_gather | solution.py:187
  156.0 23.8 %reduce-scatter.21.cloned.1.call-done = f32[64,1024]{1,0:T(8,128)} async-done(((f32[256,1024]{1,0:T(8,128)}), f32[64,1024]{1,0:T(8,128)}) %reduce-scatter.21.cloned.1.call-update) | async-done | bytes 262160 | tf_op jit(solution)/shard_map/reduce_scatter | solution.py:232
  190.7 12.8 %all_gather.54 = bf16[256,1024]{1,0:T(8,128)(2,1)S(1)} all-gather(bf16[64,1024]{1,0:T(8,128)(2,1)S(1)} %get-tuple-element.294), channel_id=1, replica_groups=mesh['section'=2,'dp'=16,'tensor'=4] {'tensor'}, dimensions={0}, use_global_device_ids=true | all-gather | bytes 655360 | tf_op jit(solution)/shard_map/all_gather | solution.py:207
  207.1 24.4 %reduce-scatter.23.cloned.1.call-done = f32[64,1024]{1,0:T(8,128)} async-done(((f32[256,1024]{1,0:T(8,128)}), f32[64,1024]{1,0:T(8,128)}) %reduce-scatter.23.cloned.1.call-update) | async-done | bytes 262160 | tf_op jit(solution)/shard_map/reduce_scatter | solution.py:220
  234.2 12.8 %all_gather.55 = bf16[256,1024]{1,0:T(8,128)(2,1)S(1)} all-gather(bf16[64,1024]{1,0:T(8,128)(2,1)S(1)} %get-tuple-element.290), channel_id=1, replica_groups=mesh['section'=2,'dp'=16,'tensor'=4] {'tensor'}, dimensions={0}, use_global_device_ids=true | all-gather | bytes 655360 | tf_op jit(solution)/shard_map/all_gather | solution.py:227
  251.4 23.4 %reduce-scatter.25.cloned.1.call-done = f32[64,1024]{1,0:T(8,128)} async-done(((f32[256,1024]{1,0:T(8,128)}), f32[64,1024]{1,0:T(8,128)}) %reduce-scatter.25.cloned.1.call-update) | async-done | bytes 262160 | tf_op jit(solution)/shard_map/reduce_scatter | solution.py:232
  286.4 12.8 %all_gather.56 = bf16[256,1024]{1,0:T(8,128)(2,1)S(1)} all-gather(bf16[64,1024]{1,0:T(8,128)(2,1)S(1)} %get-tuple-element.296), channel_id=1, replica_groups=mesh['section'=2,'dp'=16,'tensor'=4] {'tensor'}, dimensions={0}, use_global_device_ids=true | all-gather | bytes 655360 | tf_op jit(solution)/shard_map/all_gather | solution.py:207
  304.7 15.4 %all-gather.4 = bf16[1,256,1024]{2,1,0:T(8,128)(2,1)} all-gather(bf16[1,64,1024]{2,1,0:T(8,128)(2,1)S(1)} %get-tuple-element.237), channel_id=6, replica_groups=mesh['section'=2,'dp'=16,'tensor'=4] {'tensor'}, dimensions={1}, use_global_device_ids=true | all-gather | bytes 655360 | tf_op jit(solution)/shard_map/all_gather | solution.py:292
  329.9 13.4 %all_gather.57 = bf16[256,1024]{1,0:T(8,128)(2,1)S(1)} all-gather(bf16[64,1024]{1,0:T(8,128)(2,1)S(1)} %get-tuple-element.292), channel_id=1, replica_groups=mesh['section'=2,'dp'=16,'tensor'=4] {'tensor'}, dimensions={0}, use_global_device_ids=true | all-gather | bytes 655360 | tf_op jit(solution)/shard_map/all_gather | solution.py:227
  360.2 16.2 %reduce-scatter.31.cloned.1.call-done = f32[64,1024]{1,0:T(8,128)} async-done(((f32[256,1024]{1,0:T(8,128)}), f32[64,1024]{1,0:T(8,128)}) %reduce-scatter.31.cloned.1.call-update) | async-done | bytes 262160 | tf_op jit(solution)/shard_map/reduce_scatter | solution.py:297
  379.8 12.8 %all_gather.59 = bf16[256,1024]{1,0:T(8,128)(2,1)S(1)} all-gather(bf16[64,1024]{1,0:T(8,128)(2,1)S(1)} %convert_element_type.399), channel_id=1, replica_groups=mesh['section'=2,'dp'=16,'tensor'=4] {'tensor'}, dimensions={0}, use_global_device_ids=true | all-gather | bytes 655360 | tf_op jit(solution)/shard_map/all_gather | solution.py:304
  407.4 19.3 %reduce-scatter.33.cloned.1.call-done = f32[64,1024]{1,0:T(8,128)} async-done(((f32[256,1024]{1,0:T(8,128)}), f32[64,1024]{1,0:T(8,128)}) %reduce-scatter.33.cloned.1.call-update) | async-done | bytes 262160 | tf_op jit(solution)/shard_map/reduce_scatter | solution.py:317
  439.4 12.8 %all_gather.60 = bf16[256,1024]{1,0:T(8,128)(2,1)S(1)} all-gather(bf16[64,1024]{1,0:T(8,128)(2,1)S(1)} %get-tuple-element.233), channel_id=1, replica_groups=mesh['section'=2,'dp'=16,'tensor'=4] {'tensor'}, dimensions={0}, use_global_device_ids=true | all-gather | bytes 655360 | tf_op jit(solution)/shard_map/all_gather | solution.py:292
  458.4 21.4 %reduce-scatter.35.cloned.1.call-done = f32[64,1024]{1,0:T(8,128)} async-done(((f32[256,1024]{1,0:T(8,128)}), f32[64,1024]{1,0:T(8,128)}) %reduce-scatter.35.cloned.1.call-update) | async-done | bytes 262160 | tf_op jit(solution)/shard_map/reduce_scatter | solution.py:297
  483.2 13.0 %all_gather.61 = bf16[256,1024]{1,0:T(8,128)(2,1)S(1)} all-gather(bf16[64,1024]{1,0:T(8,128)(2,1)S(1)} %convert_element_type.410), channel_id=1, replica_groups=mesh['section'=2,'dp'=16,'tensor'=4] {'tensor'}, dimensions={0}, use_global_device_ids=true | all-gather | bytes 655360 | tf_op jit(solution)/shard_map/all_gather | solution.py:304
  508.9 23.3 %reduce-scatter.37.cloned.1.call-done = f32[64,1024]{1,0:T(8,128)} async-done(((f32[256,1024]{1,0:T(8,128)}), f32[64,1024]{1,0:T(8,128)}) %reduce-scatter.37.cloned.1.call-update) | async-done | bytes 262160 | tf_op jit(solution)/shard_map/reduce_scatter | solution.py:317
  568.7 17.3 %reduce-scatter.39.cloned.1.call-done = f32[64,1024]{1,0:T(8,128)} async-done(((f32[256,1024]{1,0:T(8,128)}), f32[64,1024]{1,0:T(8,128)}) %reduce-scatter.39.cloned.1.call-update) | async-done | bytes 262160 | tf_op jit(solution)/shard_map/reduce_scatter | solution.py:297
  589.4 14.2 %all_gather.63 = bf16[256,1024]{1,0:T(8,128)(2,1)S(1)} all-gather(bf16[64,1024]{1,0:T(8,128)(2,1)S(1)} %convert_element_type.418), channel_id=1, replica_groups=mesh['section'=2,'dp'=16,'tensor'=4] {'tensor'}, dimensions={0}, use_global_device_ids=true | all-gather | bytes 655360 | tf_op jit(solution)/shard_map/all_gather | solution.py:304
  654.9 277.0 %all-reduce = (f32[1,2,1024]{2,1,0:T(2,128)}, f32[1,2,1024]{2,1,0:T(2,128)}, f32[1,2,1024]{2,1,0:T(2,128)}, f32[1,2,1024]{2,1,0:T(2,128)}, f32[1,4096]{1,0:T(1,128)}) all-reduce(f32[1,2,1024]{2,1,0:T(2,128)S(1)} %fusion.251, f32[1,2,1024]{2,1,0:T(2,128)S(1)} %fusion.254, ...), channel_id=1, replica_groups=mesh['section'=2,'dp'=16,'tensor'=4] {'dp','tensor'}, use_global_device_ids=true, to_apply=%region_55.56 | all-reduce | flops 12288 | bytes 98304 | tf_op jit(solution)/shard_map/psum | solution.py:368
  (621 shorter events, 238.5 us)
Async XLA Ops:
  7.2 45.8 %all-gather.9.cloned.1.call-start = ((), (), s32[]{:S(2)}) async-start(), calls=%async_computation.31 | async-start | bytes 1671168 | tf_op jit(solution)/shard_map/all_gather | solution.py:184
  7.9 73.0 %reduce-scatter.19.cloned.1.call-start = ((), (), s32[]{:S(2)}) async-start(), calls=%async_computation.16 | async-start | bytes 1310720 | tf_op jit(solution)/shard_map/reduce_scatter | solution.py:220
  58.0 58.2 %all-gather.11.cloned.1.call-start = ((), (), s32[]{:S(2)}) async-start(), calls=%async_computation.32 | async-start | bytes 2228224 | tf_op jit(solution)/shard_map/all_gather | solution.py:186
  58.7 93.4 %all-gather.13.cloned.1.call-start = ((), (), s32[]{:S(2)}) async-start(), calls=%async_computation.33 | async-start | bytes 2228224 | tf_op jit(solution)/shard_map/all_gather | solution.py:187
  59.3 120.5 %reduce-scatter.21.cloned.1.call-start = ((), (), s32[]{:S(2)}) async-start(), calls=%async_computation.17 | async-start | bytes 1310720 | tf_op jit(solution)/shard_map/reduce_scatter | solution.py:232
  155.9 75.5 %reduce-scatter.23.cloned.1.call-start = ((), (), s32[]{:S(2)}) async-start(), calls=%async_computation.18 | async-start | bytes 1310720 | tf_op jit(solution)/shard_map/reduce_scatter | solution.py:220
  181.5 7.4 collective-permute-start
  207.0 67.8 %reduce-scatter.25.cloned.1.call-start = ((), (), s32[]{:S(2)}) async-start(), calls=%async_computation.19 | async-start | bytes 1310720 | tf_op jit(solution)/shard_map/reduce_scatter | solution.py:232
  251.4 75.8 %reduce-scatter.27.cloned.1.call-start = ((), (), s32[]{:S(2)}) async-start(), calls=%async_computation.20 | async-start | bytes 1310720 | tf_op jit(solution)/shard_map/reduce_scatter | solution.py:220
  276.5 7.4 collective-permute-start.1
  302.7 73.7 %reduce-scatter.31.cloned.1.call-start = ((), (), s32[]{:S(2)}) async-start(), calls=%async_computation.22 | async-start | bytes 1310720 | tf_op jit(solution)/shard_map/reduce_scatter | solution.py:297
  352.8 73.8 %reduce-scatter.33.cloned.1.call-start = ((), (), s32[]{:S(2)}) async-start(), calls=%async_computation.23 | async-start | bytes 1310720 | tf_op jit(solution)/shard_map/reduce_scatter | solution.py:317
  403.3 76.6 %reduce-scatter.35.cloned.1.call-start = ((), (), s32[]{:S(2)}) async-start(), calls=%async_computation.24 | async-start | bytes 1310720 | tf_op jit(solution)/shard_map/reduce_scatter | solution.py:297
  430.4 8.4 collective-permute-start.2
  457.6 74.7 %reduce-scatter.37.cloned.1.call-start = ((), (), s32[]{:S(2)}) async-start(), calls=%async_computation.25 | async-start | bytes 1310720 | tf_op jit(solution)/shard_map/reduce_scatter | solution.py:317
  508.9 77.1 %reduce-scatter.39.cloned.1.call-start = ((), (), s32[]{:S(2)}) async-start(), calls=%async_computation.26 | async-start | bytes 1310720 | tf_op jit(solution)/shard_map/reduce_scatter | solution.py:297
  536.0 8.4 collective-permute-start.3
  564.0 86.6 %reduce-scatter.29.cloned.1.call-start = ((), (), s32[]{:S(2)}) async-start(), calls=%async_computation.21 | async-start | bytes 1310720 | tf_op jit(solution)/shard_map/reduce_scatter | solution.py:232
  568.6 85.0 %reduce-scatter.41.cloned.1.call-start = ((), (), s32[]{:S(2)}) async-start(), calls=%async_computation.27 | async-start | bytes 1310720 | tf_op jit(solution)/shard_map/reduce_scatter | solution.py:317
  614.8 319.1 %reduce-scatter.49.cloned.1.call-start = ((), (), s32[]{:S(2)}) async-start(), calls=%async_computation.34 | async-start | bytes 4456448
  626.8 309.2 %reduce-scatter.45.cloned.1.call-start = ((), (), s32[]{:S(2)}) async-start(), calls=%async_computation.29 | async-start | bytes 1114112 | tf_op jit(solution)/shard_map/reduce_scatter | solution.py:361
  630.4 305.5 %reduce-scatter.43.cloned.1.call-start = ((), (), s32[]{:S(2)}) async-start(), calls=%async_computation.28 | async-start | bytes 3342336 | tf_op jit(solution)/shard_map/reduce_scatter | solution.py:360
  642.9 293.1 %reduce-scatter.47.cloned.1.call-start = ((), (), s32[]{:S(2)}) async-start(), calls=%async_computation.30 | async-start | bytes 4456448 | tf_op jit(solution)/shard_map/reduce_scatter | solution.py:362
  649.9 283.1 %copy-start.78 = (f32[64,1024]{1,0:T(8,128)S(1)}, f32[64,1024]{1,0:T(8,128)}, u32[]{:S(2)}) copy-start(f32[64,1024]{1,0:T(8,128)} %get-tuple-element.241) | copy-start | bytes 786436
  (172 other events, 2699.3 us)
Sparse Core Ops, SparseCore 0:
  9.7 36.3 all-gather.8
  58.1 22.7 reduce-scatter.18
  82.8 33.3 all-gather.10
  117.9 34.2 all-gather.12
  156.1 23.7 reduce-scatter.20
  207.1 24.2 reduce-scatter.22
  251.5 23.2 reduce-scatter.24
  302.8 24.3 reduce-scatter.26
  353.0 23.4 reduce-scatter.30
  403.4 23.2 reduce-scatter.32
  457.7 22.0 reduce-scatter.34
  509.0 23.2 reduce-scatter.36
  564.1 21.8 reduce-scatter.38
  588.2 23.7 reduce-scatter.28
  614.9 23.0 reduce-scatter.40
  640.3 67.0 reduce-scatter.48
  710.2 60.0 reduce-scatter.44
  773.3 64.0 reduce-scatter.42
  840.5 65.9 reduce-scatter.46
where the time goes:
time: 953 us; the launch traced here: 943 us
  blocking collectives  459 us (48%)
  waiting for transfers between devices  263 us (28%)
  matrix products  79.3 us (8%)
  other arithmetic  65.6 us (7%)
  local copies, waits for them, and re-layouts  46.1 us (5%)
  between operations  16.6 us (2%)
  starting transfers between devices  13.4 us (1%)
    psum x1, blocking collectives, local(): lax.psum((small_sums[0], small_sums[1], small_sums[2], small_sums[3], sma...  277 us
    reduce_scatter x3, waiting for transfers between devices, local(): lax.psum_scatter(dot_cols(grad_before_low, fc1_full), 'tensor', scatter_d...  54.9 us
    reduce_scatter x3, waiting for transfers between devices, local(): lax.psum_scatter(dot_plain(forward_active_low, fc2_full), 'tensor', scatt...  47.2 us
    reduce_scatter x3, waiting for transfers between devices, local(): lax.psum_scatter(dot_plain(forward_mixed_rows, out_full), 'tensor', scatt...  46 us
    reduce_scatter x3, waiting for transfers between devices, local(): lax.psum_scatter(dot_cols(grad_proj, qkv_flat), 'tensor', scatter_dimensi...  42.7 us
    all_gather x3, blocking collectives, local(): lax.all_gather(grad_out.astype(jnp.bfloat16), 'tensor', axis=0, tiled=True)  40.9 us
    all_gather x3, blocking collectives, local(): lax.all_gather(normed_two.astype(jnp.bfloat16), 'tensor', axis=0, tiled=T...  40.1 us
    all_gather x3, blocking collectives, local(): lax.all_gather(grad_middle.astype(jnp.bfloat16), 'tensor', axis=0, tiled=...  40 us
  transfers between devices with their start and end apart: 23, of which 16 were waited for; matrix products, arithmetic and copies ran while one was open for 10% of the time, Pallas kernels for 0%

commit v1 on v0

v1 whole, which is shorter than its diff:
```python
import functools
import math

import jax
import jax.numpy as jnp
from jax import lax
from jax.experimental import pallas as pl
from jax.experimental.pallas import tpu as pltpu
from jax.sharding import PartitionSpec as P

D = 1024
HD = 64
FF = 4096
SEQ = 256
ROWS = 64
WIDE = 3072
NEGATIVE = -1000000000.0
GELU_COEF = 0.7978845608028654
EPSILON = 1e-05
MESH = pl.DeviceIdType.MESH
BF16 = jnp.bfloat16
F32 = jnp.float32

GAIN, OFFSET, PROJ, QV, FC = 0, 2, 4, 6, 8
SMALL = 16


def dot_nn(a, b):
    return lax.dot_general(a, b, (((1,), (0,)), ((), ())), preferred_element_type=F32)


def dot_nt(a, b):
    return lax.dot_general(a, b, (((1,), (1,)), ((), ())), preferred_element_type=F32)


def dot_tn(a, b):
    return lax.dot_general(a, b, (((0,), (0,)), ((), ())), preferred_element_type=F32)


def norm_rows(hidden, gain_row, offset_row):
    centre = hidden - jnp.mean(hidden, axis=-1, keepdims=True)
    spread = jnp.mean(centre * centre, axis=-1, keepdims=True)
    inverse = lax.rsqrt(spread + EPSILON)
    unit_rows = centre * inverse
    return unit_rows * gain_row + offset_row, unit_rows, inverse


def norm_back(grad_rows, unit_rows, inverse, gain_row):
    grad_unit = grad_rows * gain_row
    return inverse * (
        grad_unit
        - jnp.mean(grad_unit, axis=-1, keepdims=True)
        - unit_rows * jnp.mean(grad_unit * unit_rows, axis=-1, keepdims=True)
    )


def row_sum(value):
    return jnp.sum(value, axis=0, keepdims=True)


def kernel(
    x_ref, cot_ref, seg_ref, shard_ref, gain_ref, offset_ref, qv_ref, proj_ref, fc_ref,
    out_ref, grad_ref, wgrad_ref, small_ref,
    w, gd, r0, r1, r2, p1, pb,
    g1, g2, gm, ga, sbuf, rbuf,
    qkv_s, prob_s, mixed_s, active_s, slope_s, unit_s, inv_s, mid_s,
    gb_s, gp_s, gt_s, mask_s, dy_s, xs, xr, sm, arm, arx, ary, arz,
    z_send, z_recv, gy_send, gy_recv, gx_send, gx_recv, gc_send, gc_recv,
    rc_send, rc_recv, rx_send, rx_recv, ry_send, ry_recv, o_send, o_recv, a_send, a_recv,
):
    s = lax.axis_index("section")
    d = lax.axis_index("dp")
    t = lax.axis_index("tensor")
    x = d // 4
    yl = (d // 2) % 2
    c = d % 2
    y = 2 * s + yl
    mate = {"section": s, "dp": d + 1 - 2 * c, "tensor": t}
    zp = [{"section": s, "dp": d, "tensor": (t + k) % 4} for k in (1, 2, 3)]
    xp = [{"section": s, "dp": ((x + k) % 4) * 4 + yl * 2 + c, "tensor": t} for k in (1, 2, 3)]
    yp = []
    for k in (1, 2, 3):
        other = (y + k) % 4
        yp.append({"section": other // 2, "dp": x * 4 + (other % 2) * 2 + c, "tensor": t})
    across = {"section": 1 - s, "dp": d, "tensor": t}

    def remote(src, dst, send, recv, peer):
        return pltpu.make_async_remote_copy(
            src_ref=src, dst_ref=dst, send_sem=send, recv_sem=recv, device_id=peer, device_id_type=MESH
        )

    pending = {}

    def begin(key, copy, cond=None):
        if cond is None:
            copy.start()
        else:
            pl.when(cond)(copy.start)
        pending.setdefault(key, []).append((copy, cond))

    def flush(key):
        for copy, cond in pending.pop(key, []):
            if cond is None:
                copy.wait_send()
            else:
                pl.when(cond)(copy.wait_send)

    barrier = pltpu.get_barrier_semaphore()
    for peer in zp + xp + yp + [mate]:
        pl.semaphore_signal(barrier, inc=1, device_id=peer, device_id_type=MESH)
    pl.semaphore_wait(barrier, 10)

    def cols(g):
        return pl.ds(g * 1024, 1024)

    def gather_y(g):
        for k in (1, 2, 3):
            begin("gy", remote(
                shard_ref.at[:, cols(g)], w.at[s, 2 * x + yl, c, :, cols(g)],
                gy_send.at[g, k - 1], gy_recv.at[s, g, k - 1], yp[k - 1],
            ))

    def gather_x(l, g):
        for k in (1, 2, 3):
            src_y = (y - k + 4) % 4
            copy = remote(
                shard_ref.at[:, cols(g)], w.at[l, 2 * x + src_y % 2, c, :, cols(g)],
                gy_send.at[g, k - 1], gy_recv.at[l, g, k - 1], yp[k - 1],
            )
            pl.when(src_y // 2 == l)(copy.wait_recv)
        mine = w.at[l, pl.ds(2 * x, 2), c, :, cols(g)]
        for k in (1, 2, 3):
            begin("gx", remote(mine, mine, gx_send.at[l, g, k - 1], gx_recv.at[l, g, k - 1], xp[k - 1]))

    def gather_c(l, g):
        for k in (1, 2, 3):
            theirs = w.at[l, pl.ds(2 * ((x - k + 4) % 4), 2), c, :, cols(g)]
            remote(theirs, theirs, gx_send.at[l, g, k - 1], gx_recv.at[l, g, k - 1], xp[k - 1]).wait_recv()
        half = w.at[l, :, c, :, cols(g)]
        begin("gc", remote(half, half, gc_send.at[l, g], gc_recv.at[l, g], mate))

    def gather_done(l, g):
        half = w.at[l, :, 1 - c, :, cols(g)]
        remote(half, half, gc_send.at[l, g], gc_recv.at[l, g], mate).wait_recv()

    def reduce_c(l, g):
        begin(("rc", l, g), remote(
            gd.at[:, 1 - c, :, cols(g)], r0.at[l, :, :, cols(g)], rc_send.at[l, g], rc_recv.at[l, g], mate
        ))

    def reduce_x(l, g):
        remote(
            gd.at[:, 1 - c, :, cols(g)], r0.at[l, :, :, cols(g)], rc_send.at[l, g], rc_recv.at[l, g], mate
        ).wait_recv()

        def add(i, _):
            gd[i, c, :, cols(g)] = (
                gd[i, c, :, cols(g)].astype(F32) + r0[l, i, :, cols(g)].astype(F32)
            ).astype(BF16)
            return 0

        lax.fori_loop(0, 8, add, 0)
        for k in (1, 2, 3):
            begin(("rx", l, g), remote(
                gd.at[pl.ds(2 * ((x + k) % 4), 2), c, :, cols(g)], r1.at[l, k - 1, :, :, cols(g)],
                rx_send.at[l, g, k - 1], rx_recv.at[l, g, k - 1], xp[k - 1],
            ))

    def reduce_y(l, g):
        for k in (1, 2, 3):
            remote(
                gd.at[pl.ds(2 * ((x + k) % 4), 2), c, :, cols(g)], r1.at[l, k - 1, :, :, cols(g)],
                rx_send.at[l, g, k - 1], rx_recv.at[l, g, k - 1], xp[k - 1],
            ).wait_recv()
        for half in (0, 1):
            total = gd[2 * x + half, c, :, cols(g)].astype(F32)
            for k in (0, 1, 2):
                total += r1[l, k, half, :, cols(g)].astype(F32)
            p1[l, half, :, cols(g)] = total.astype(BF16)
        for k in (1, 2, 3):
            target = (y + k) % 4
            begin("ry", remote(
                p1.at[l, target % 2, :, cols(g)], r2.at[l, k - 1, :, cols(g)],
                ry_send.at[l, g, k - 1], ry_recv.at[l, g, k - 1], yp[k - 1],
            ), target // 2 == l)

    def reduce_done(l, g):
        copies = [
            remote(
                p1.at[l, 0, :, cols(g)], r2.at[l, k, :, cols(g)],
                ry_send.at[l, g, k], ry_recv.at[l, g, k], yp[k],
            )
            for k in (0, 1, 2)
        ]

        @pl.when(s == l)
        def _():
            for copy in copies:
                copy.wait_recv()
            total = p1[l, yl, :, cols(g)].astype(F32)
            for k in (0, 1, 2):
                total += r2[l, k, :, cols(g)].astype(F32)
            wgrad_ref[:, cols(g)] = total

    def spread_start(event, buf):
        for k in (1, 2, 3):
            begin("z", remote(buf.at[t], buf.at[t], z_send.at[event, k - 1], z_recv.at[event, k - 1], zp[k - 1]))

    def spread_done(event, buf):
        for k in (1, 2, 3):
            theirs = buf.at[(t - k + 4) % 4]
            remote(theirs, theirs, z_send.at[event, k - 1], z_recv.at[event, k - 1], zp[k - 1]).wait_recv()

    def sum_start(event):
        slot = event % 2
        for k in (1, 2, 3):
            begin(("s", slot), remote(
                sbuf.at[slot, (t + k) % 4], rbuf.at[event, k - 1],
                z_send.at[event, k - 1], z_recv.at[event, k - 1], zp[k - 1],
            ))

    def sum_done(event):
        slot = event % 2
        for k in (1, 2, 3):
            remote(
                sbuf.at[slot, (t + k) % 4], rbuf.at[event, k - 1],
                z_send.at[event, k - 1], z_recv.at[event, k - 1], zp[k - 1],
            ).wait_recv()
        total = sbuf[slot, t].astype(F32)
        for k in (0, 1, 2):
            total += rbuf[event, k].astype(F32)
        return total

    def share(event, lhs, l, c0, n):
        slot = event % 2
        flush(("s", slot))

        def tile(j, _):
            right = w[l, pl.ds(2 * j, 2), :, :, pl.ds(c0, n)].reshape(256, n)
            part = dot_nt(lhs(), right).astype(BF16)
            sbuf[slot, :, :, pl.ds(pl.multiple_of(j * 256, 256), 256)] = part.reshape(4, 64, 256)
            return 0

        lax.fori_loop(0, 4, tile, 0)

    def weight_grad(lhs_ref, rhs, c0, n):
        def turn(i, _):
            piece = lhs_ref[:, :, pl.ds(pl.multiple_of(i * 256, 256), 256)].reshape(256, 256)
            gt_s[pl.ds(pl.multiple_of(i * 256, 256), 256), :] = piece.T
            return 0

        lax.fori_loop(0, 4, turn, 0)

        def tile(step, _):
            i, j = step // (n // 256), step % (n // 256)
            left = gt_s[pl.ds(pl.multiple_of(i * 256, 256), 256), :]
            part = dot_nn(left, rhs[:, pl.ds(pl.multiple_of(j * 256, 256), 256)])
            gd[pl.ds(2 * i, 2), :, :, pl.ds(pl.multiple_of(c0 + j * 256, 256), 256)] = part.astype(
                BF16
            ).reshape(2, 2, 64, 256)
            return 0

        lax.fori_loop(0, 4 * (n // 256), tile, 0)

    def cross_send(index, value, l, local_ref):
        @pl.when(s == l)
        def _():
            local_ref[s] = value

        @pl.when(s != l)
        def _():
            xs[index] = value

        begin("o", remote(xs.at[index], xr.at[index], o_send.at[index], o_recv.at[index], across), s != l)

    gather_y(0)
    pb[s, GAIN:GAIN + 2] = gain_ref[...]
    pb[s, OFFSET:OFFSET + 2] = offset_ref[...]
    pb[s, PROJ:PROJ + 2] = proj_ref[...]
    pb[s, QV:QV + 2] = qv_ref[...]
    for k in range(4):
        pb[s, FC + k:FC + k + 1] = fc_ref[:, k * 1024:(k + 1) * 1024]
    pb[s, FC + 4:] = jnp.zeros((SMALL - FC - 4, D), F32)
    begin("pb", remote(pb.at[s], pb.at[s], o_send.at[2], o_recv.at[2], across))
    gm[1, t] = cot_ref[s]
    spread_start(8, gm.at[1])
    w[s, 2 * x + yl, c] = shard_ref[...]
    sm[...] = jnp.zeros_like(sm)
    seg_rows = jnp.broadcast_to(seg_ref[s].astype(F32), (SEQ, SEQ))
    seg_cols = seg_rows.T
    places_i = lax.broadcasted_iota(jnp.int32, (SEQ, SEQ), 0)
    places_j = lax.broadcasted_iota(jnp.int32, (SEQ, SEQ), 1)
    mask_s[...] = jnp.where((seg_rows == seg_cols) & (places_i >= places_j), 1.0, 0.0)
    remote(pb.at[1 - s], pb.at[1 - s], o_send.at[2], o_recv.at[2], across).wait_recv()

    def small(l, row):
        return pb[l, row:row + 1]

    def forward(l, hidden, pump):
        normed, unit, inverse = norm_rows(hidden, small(l, GAIN), small(l, OFFSET))
        unit_s[l, 0] = unit
        inv_s[l, 0] = inverse
        g1[l, t] = normed.astype(BF16)
        spread_start(4 * l, g1.at[l])
        mid_s[...] = hidden
        pump(0)
        spread_done(4 * l, g1.at[l])
        gather_done(l, 0)
        for j in range(3):
            part = dot_nn(
                g1[l].reshape(SEQ, D), w[l, :, :, :, j * 256:(j + 1) * 256].reshape(D, 256)
            )
            if j != 1:
                part = part + pb[l, QV + j // 2:QV + j // 2 + 1, pl.ds(pl.multiple_of(t * 256, 256), 256)]
            qkv_s[l, :, j * 256:(j + 1) * 256] = part.astype(BF16)
        pump(1)
        for pair in range(2):
            mixed = []
            for n in (2 * pair, 2 * pair + 1):
                lo = n * HD
                scores = dot_nt(qkv_s[l, :, lo:lo + HD], qkv_s[l, :, 256 + lo:256 + lo + HD]) * 0.125
                scores = jnp.where(mask_s[...] > 0.5, scores, NEGATIVE)
                shifted = jnp.exp(scores - jnp.max(scores, axis=-1, keepdims=True))
                probs = shifted / jnp.sum(shifted, axis=-1, keepdims=True)
                prob_s[l, n] = probs
                mixed.append(dot_nn(probs.astype(BF16), qkv_s[l, :, 512 + lo:512 + lo + HD]))
            mixed_s[l, :, pair * 128:(pair + 1) * 128] = jnp.concatenate(mixed, axis=1).astype(BF16)
        share(4 * l + 1, lambda: mixed_s[l], l, 768, 256)
        sum_start(4 * l + 1)
        pump(2)
        middle = mid_s[...] + (sum_done(4 * l + 1) + small(l, PROJ))
        normed, unit, inverse = norm_rows(middle, small(l, GAIN + 1), small(l, OFFSET + 1))
        unit_s[l, 1] = unit
        inv_s[l, 1] = inverse
        g2[l, t] = normed.astype(BF16)
        spread_start(4 * l + 2, g2.at[l])
        mid_s[...] = middle
        pump(3)
        spread_done(4 * l + 2, g2.at[l])
        gather_done(l, 1)

        def up(j, _):
            at = pl.ds(pl.multiple_of(j * 256, 256), 256)
            before = dot_nn(
                g2[l].reshape(SEQ, D),
                w[l, :, :, :, pl.ds(pl.multiple_of(1024 + j * 256, 256), 256)].reshape(D, 256),
            ) + pb[l, pl.ds(FC + t, 1), at]
            tanh_part = jnp.tanh(GELU_COEF * (before + 0.044715 * before * before * before))
            active_s[l, :, at] = (0.5 * before * (1.0 + tanh_part)).astype(BF16)
            slope_s[l, :, at] = 0.5 * (1.0 + tanh_part) + 0.5 * before * (
                1.0 - tanh_part * tanh_part
            ) * GELU_COEF * (1.0 + 3.0 * 0.044715 * before * before)
            return 0

        lax.fori_loop(0, 4, up, 0)
        pump(4)
        gather_done(l, 2)
        share(4 * l + 3, lambda: active_s[l], l, 2048, 1024)
        sum_start(4 * l + 3)
        pump(5)
        return mid_s[...] + (sum_done(4 * l + 3) + small(l, PROJ + 1))

    def backward(l, pump):
        event = 8 + 4 * (1 - l)
        row = l * SMALL
        sm[row + PROJ + 1:row + PROJ + 2] = row_sum(dy_s[...])
        spread_done(event, gm.at[l])

        def down(j, _):
            at = pl.ds(pl.multiple_of(j * 256, 256), 256)
            grad_before = dot_nn(
                gm[l].reshape(SEQ, D),
                w[l, :, :, :, pl.ds(pl.multiple_of(2048 + j * 256, 256), 256)].reshape(D, 256),
            ) * slope_s[l, :, at]
            sm[pl.ds(row + FC + t, 1), at] = row_sum(grad_before)
            gb_s[:, at] = grad_before.astype(BF16)
            return 0

        lax.fori_loop(0, 4, down, 0)
        share(event + 1, lambda: gb_s[...], l, 1024, 1024)
        sum_start(event + 1)
        pump(0)
        weight_grad(gm.at[l], active_s.at[l], 2048, 1024)
        reduce_c(l, 2)
        weight_grad(g2.at[l], gb_s, 1024, 1024)
        reduce_c(l, 1)
        pump(1)
        grad = sum_done(event + 1)
        sm[row + GAIN + 1:row + GAIN + 2] = row_sum(grad * unit_s[l, 1])
        sm[row + OFFSET + 1:row + OFFSET + 2] = row_sum(grad)
        grad_middle = dy_s[...] + norm_back(grad, unit_s[l, 1], inv_s[l, 1], small(l, GAIN + 1))
        dy_s[...] = grad_middle
        ga[l, t] = grad_middle.astype(BF16)
        spread_start(event + 2, ga.at[l])
        sm[row + PROJ:row + PROJ + 1] = row_sum(grad_middle)
        pump(2)
        spread_done(event + 2, ga.at[l])
        grad_mixed = dot_nn(
            ga[l].reshape(SEQ, D), w[l, :, :, :, 768:1024].reshape(D, 256)
        ).astype(BF16)
        for pair in range(2):
            grads = [[], [], []]
            for n in (2 * pair, 2 * pair + 1):
                lo = n * HD
                q = qkv_s[l, :, lo:lo + HD]
                key = qkv_s[l, :, 256 + lo:256 + lo + HD]
                value = qkv_s[l, :, 512 + lo:512 + lo + HD]
                grad_head = grad_mixed[:, lo:lo + HD]
                probs = prob_s[l, n]
                grad_probs = dot_nt(grad_head, value)
                row_dot = jnp.sum(probs * grad_probs, axis=-1, keepdims=True)
                grad_scores = (probs * (grad_probs - row_dot)).astype(BF16)
                grads[0].append(dot_nn(grad_scores, key) * 0.125)
                grads[1].append(dot_tn(grad_scores, q) * 0.125)
                grads[2].append(dot_tn(probs.astype(BF16), grad_head))
            for j in range(3):
                both = jnp.concatenate(grads[j], axis=1)
                gp_s[:, j * 256 + pair * 128:j * 256 + (pair + 1) * 128] = both.astype(BF16)
                if j != 1:
                    sm[
                        row + QV + j // 2:row + QV + j // 2 + 1,
                        pl.ds(pl.multiple_of(t * 256 + pair * 128, 128), 128),
                    ] = row_sum(both)
        share(event + 3, lambda: gp_s[...], l, 0, 768)
        sum_start(event + 3)
        pump(3)
        weight_grad(ga.at[l], mixed_s.at[l], 768, 256)
        weight_grad(g1.at[l], gp_s, 0, 768)
        reduce_c(l, 0)
        pump(4)
        grad = sum_done(event + 3)
        sm[row + GAIN:row + GAIN + 1] = row_sum(grad * unit_s[l, 0])
        sm[row + OFFSET:row + OFFSET + 1] = row_sum(grad)
        return dy_s[...] + norm_back(grad, unit_s[l, 0], inv_s[l, 0], small(l, GAIN))

    def pump_f0(i):
        if i == 0:
            gather_x(0, 0)
            gather_y(1)
            gather_c(0, 0)
            gather_x(0, 1)
            gather_y(2)
        if i == 2:
            gather_c(0, 1)
            gather_x(0, 2)
        if i == 4:
            gather_c(0, 2)
            gather_x(1, 0)

    def pump_f1(i):
        if i == 0:
            gather_c(1, 0)
            gather_x(1, 1)
        if i == 2:
            gather_c(1, 1)
            gather_x(1, 2)
        if i == 4:
            gather_c(1, 2)

    hidden = forward(0, x_ref[s].astype(F32), pump_f0)
    cross_send(0, hidden, 0, out_ref)
    hidden = forward(1, hidden.astype(BF16).astype(F32), pump_f1)
    cross_send_late = hidden

    def pump_b1(i):
        if i == 2:
            reduce_x(1, 2)
        if i == 3:
            reduce_y(1, 2)
            reduce_x(1, 1)

    def pump_b0(i):
        if i == 0:
            reduce_y(1, 1)
            reduce_x(1, 0)
            for g in (1, 2):
                flush(("rc", 1, g))
                flush(("rx", 1, g))
        if i == 2:
            reduce_y(1, 0)
            reduce_x(0, 2)
        if i == 3:
            reduce_y(0, 2)
            reduce_x(0, 1)
            flush(("rc", 1, 0))
            flush(("rx", 1, 0))
        if i == 4:
            reduce_y(0, 1)
            reduce_x(0, 0)

    dy_s[...] = cot_ref[s].astype(F32)
    @pl.when(s == 1)
    def _():
        out_ref[s] = cross_send_late

    @pl.when(s == 0)
    def _():
        xs[0] = cross_send_late

    begin("o", remote(xs.at[0], xr.at[0], o_send.at[0], o_recv.at[0], across), s == 0)

    grad = backward(1, pump_b1).astype(BF16)
    dy_s[...] = grad.astype(F32)
    gm[0, t] = grad
    spread_start(12, gm.at[0])
    cross_send(1, grad.astype(F32), 1, grad_ref)
    grad = backward(0, pump_b0)

    @pl.when(s == 0)
    def _():
        grad_ref[s] = grad

    @pl.when(s == 1)
    def _():
        xs[1] = grad

    begin("o", remote(xs.at[1], xr.at[1], o_send.at[1], o_recv.at[1], across), s == 1)

    a_at = 0
    value = sm[...]
    for buf, me, peers in (
        (arm, c, [mate]), (arx, x, xp), (ary, y, yp), (arz, t, zp)
    ):
        n = len(peers) + 1
        buf[me] = value
        for k in range(1, n):
            begin("a", remote(buf.at[me], buf.at[me], a_send.at[a_at + k], a_recv.at[a_at + k], peers[k - 1]))
        if buf is arm:
            reduce_y(0, 0)
        for k in range(1, n):
            theirs = buf.at[(me - k + n) % n]
            remote(theirs, theirs, a_send.at[a_at + k], a_recv.at[a_at + k], peers[k - 1]).wait_recv()
        value = buf[0]
        for k in range(1, n):
            value = value + buf[k]
        a_at += 4
    small_ref[...] = jnp.where(s == 0, value[:SMALL], value[SMALL:])
    for l in (1, 0):
        for g in (2, 1, 0):
            reduce_done(l, g)
    for index, ref in ((0, out_ref), (1, grad_ref)):
        remote(xs.at[index], xr.at[index], o_send.at[index], o_recv.at[index], across).wait_recv()
        ref[1 - s] = xr[index]
    for key in list(pending):
        flush(key)


def fused(x, cot, seg, shard, gains, offsets, qv, proj, fc):
    vmem = pl.BlockSpec(memory_space=pltpu.VMEM)
    dma = pltpu.SemaphoreType.DMA
    scratch = [
        pltpu.VMEM((2, 8, 2, ROWS, WIDE), BF16),
        pltpu.VMEM((8, 2, ROWS, WIDE), BF16),
        pltpu.VMEM((2, 8, ROWS, WIDE), BF16),
        pltpu.VMEM((2, 3, 2, ROWS, WIDE), BF16),
        pltpu.VMEM((2, 3, ROWS, WIDE), BF16),
        pltpu.VMEM((2, 2, ROWS, WIDE), BF16),
        pltpu.VMEM((2, SMALL, D), F32),
        pltpu.VMEM((2, 4, ROWS, D), BF16),
        pltpu.VMEM((2, 4, ROWS, D), BF16),
        pltpu.VMEM((2, 4, ROWS, D), BF16),
        pltpu.VMEM((2, 4, ROWS, D), BF16),
        pltpu.VMEM((2, 4, ROWS, D), BF16),
        pltpu.VMEM((16, 3, ROWS, D), BF16),
        pltpu.VMEM((2, SEQ, 768), BF16),
        pltpu.VMEM((2, 4, SEQ, SEQ), F32),
        pltpu.VMEM((2, SEQ, 256), BF16),
        pltpu.VMEM((2, SEQ, D), BF16),
        pltpu.VMEM((2, SEQ, D), F32),
        pltpu.VMEM((2, 2, ROWS, D), F32),
        pltpu.VMEM((2, 2, ROWS, 1), F32),
        pltpu.VMEM((ROWS, D), F32),
        pltpu.VMEM((SEQ, D), BF16),
        pltpu.VMEM((SEQ, 768), BF16),
        pltpu.VMEM((D, SEQ), BF16),
        pltpu.VMEM((SEQ, SEQ), F32),
        pltpu.VMEM((ROWS, D), F32),
        pltpu.VMEM((2, ROWS, D), F32),
        pltpu.VMEM((2, ROWS, D), F32),
        pltpu.VMEM((2 * SMALL, D), F32),
        pltpu.VMEM((2, 2 * SMALL, D), F32),
        pltpu.VMEM((4, 2 * SMALL, D), F32),
        pltpu.VMEM((4, 2 * SMALL, D), F32),
        pltpu.VMEM((4, 2 * SMALL, D), F32),
        dma((16, 3)), dma((16, 3)),
        dma((3, 3)), dma((2, 3, 3)),
        dma((2, 3, 3)), dma((2, 3, 3)),
        dma((2, 3)), dma((2, 3)),
        dma((2, 3)), dma((2, 3)),
        dma((2, 3, 3)), dma((2, 3, 3)),
        dma((2, 3, 3)), dma((2, 3, 3)),
        dma((3,)), dma((3,)),
        dma((16,)), dma((16,)),
    ]
    return pl.pallas_call(
        kernel,
        out_shape=(
            jax.ShapeDtypeStruct((2, ROWS, D), F32),
            jax.ShapeDtypeStruct((2, ROWS, D), F32),
            jax.ShapeDtypeStruct((ROWS, WIDE), F32),
            jax.ShapeDtypeStruct((SMALL, D), F32),
        ),
        in_specs=[vmem] * 9,
        out_specs=(vmem,) * 4,
        scratch_shapes=scratch,
        compiler_params=pltpu.CompilerParams(
            collective_id=0, has_side_effects=True, vmem_limit_bytes=62 * 2**20
        ),
    )(x, cot, seg, shard, gains, offsets, qv, proj, fc)


def local(
    inputs, cotangent, segments, qkv_weight, out_weight, fc1_weight, fc2_weight,
    ln_gains, ln_biases, qv_bias, proj_biases, fc_bias,
):
    shard = jnp.concatenate(
        [qkv_weight[0].reshape(ROWS, 768), out_weight[0].T, fc1_weight[0], fc2_weight[0].T], axis=1
    )
    outs, grads, wgrad, small = fused(
        inputs, cotangent, segments, shard, ln_gains[0], ln_biases[0], qv_bias[0], proj_biases[0], fc_bias
    )
    return (
        outs[None],
        grads[None],
        wgrad[:, :768].reshape(1, ROWS, 3, 256),
        wgrad[:, 768:1024].T[None],
        wgrad[:, 1024:2048][None],
        wgrad[:, 2048:].T[None],
        small[GAIN:GAIN + 2][None],
        small[OFFSET:OFFSET + 2][None],
        small[QV:QV + 2][None],
        small[PROJ:PROJ + 2][None],
        small[FC:FC + 4].reshape(1, FF),
    )


def solution(mesh):
    in_specs = (
        P(None, ("dp", "tensor"), None),
        P(None, ("dp", "tensor"), None),
        P(None, "dp", None),
        P("section", "dp", None, "tensor"),
        P("section", "tensor", "dp"),
        P("section", "dp", "tensor"),
        P("section", "tensor", "dp"),
        P("section", None, None),
        P("section", None, None),
        P("section", None, None),
        P("section", None, None),
        P("section", None),
    )
    out_specs = (
        P("section", None, ("dp", "tensor"), None),
        P("section", None, ("dp", "tensor"), None),
        P("section", "dp", None, "tensor"),
        P("section", "tensor", "dp"),
        P("section", "dp", "tensor"),
        P("section", "tensor", "dp"),
        P("section", None, None),
        P("section", None, None),
        P("section", None, None),
        P("section", None, None),
        P("section", None),
    )
    return jax.shard_map(local, mesh=mesh, in_specs=in_specs, out_specs=out_specs, check_vma=False)
```

time: 953 us -> 243 us (0.25)
  blocking collectives: 459 us -> 0 us
  waiting for transfers between devices: 263 us -> 0 us
  Pallas kernels: 0 us -> 227 us
  matrix products: 79.3 us -> 0 us
  other arithmetic: 65.6 us -> 0.77 us
  local copies, waits for them, and re-layouts: 46.1 us -> 12.1 us
  between operations: 16.6 us -> 0.71 us
  starting transfers between devices: 13.4 us -> 0 us
    psum x1 -> x0, blocking collectives: 277 us -> none  [local(): lax.psum((small_sums[0], small_sums[1], small_sums[2], small_sums[3], sma...]
    pallas_call x0 -> x1, Pallas kernels: none -> 227 us  [fused(): pl.pallas_call(kernel, out_shape=(jax.ShapeDtypeStruct((2, ROWS, D), F32)...]
    reduce_scatter x15 -> x0, waiting for transfers between devices: 191 us -> none  [the longest x3 54.9 us: local(): lax.psum_scatter(dot_cols(grad_before_low, fc1_full), 'tensor', scatter_d...]
    all_gather x13 -> x0, blocking collectives: 182 us -> none  [the longest x3 40.9 us: local(): lax.all_gather(grad_out.astype(jnp.bfloat16), 'tensor', axis=0, tiled=True)]
    dot_general x57 -> x0, matrix products: 79.3 us -> none  [the longest x12 21.3 us: dot_cols(): lax.dot_general(left_side, right_side, (((1,), (1,)), ((), ())), preferre...]
    all_gather x3 -> x0, waiting for transfers between devices: 51.1 us -> none  [the longest x1 32.4 us: local(): lax.all_gather(fc2_weight[0], 'dp', axis=1, tiled=True)]
    reduce_sum x27 -> x0, other arithmetic: 25 us -> none  [the longest x6 9.69 us: norm_back(): jnp.sum(grad_rows * unit_rows, axis=0)]
    another operation x24 -> x0, other arithmetic: 19 us -> none  [the longest x22 16.9 us: local(): saved_all = jax.tree.map(lambda *leaves: jnp.stack(leaves), *saved_ticks)]
  transfers between devices with their start and end apart: 23 -> 0, of which waited for: 16 -> 0; matrix products, arithmetic and copies ran while one was open for 10% -> 0% of each run, Pallas kernels for 0% -> 0%
where the time goes in v1:
time: 243 us; the launch traced here: 241 us
  Pallas kernels  227 us (93%)
  local copies, waits for them, and re-layouts  12.1 us (5%)
    pallas_call x1, Pallas kernels, fused(): pl.pallas_call(kernel, out_shape=(jax.ShapeDtypeStruct((2, ROWS, D), F32)...  227 us
    unnamed x17, local copies, waits for them, and re-layouts  6.23 us

profile of v1, /device:TPU:0, one launch (start us, length us, event | category | flops | bytes accessed | tf_op | source)
XLA Modules:
  0.0 241.1 jit_solution(16331726083591316715)
XLA Ops:
  0.6 0.0 copy-start.3
  0.7 1.0 copy.25
  1.7 0.0 copy-start.2
  1.7 0.0 copy-start.4
  1.7 0.0 copy-done.3
  1.7 0.9 copy-done.2
  2.6 0.0 copy-done.4
  2.6 0.8 pad_maximum_fusion.shard_ref
  3.4 227.5 %shard_map.203 = (f32[2,64,1024]{2,1,0:T(8,128)}, f32[2,64,1024]{2,1,0:T(8,128)}, f32[64,3072]{1,0:T(8,128)}, f32[16,1024]{1,0:T(8,128)}) custom-call(bf16[2,64,1024]{2,1,0:T(8,128)(2,1)} %x_ref.1, bf16[2,64,1024]{2,1,0:T(8,128)(2,1)} %cot_ref.1, s32[2,1,256]{2,1,0:T(1,128)} %seg_ref.1, bf16[64,3072]{1,0:T(8,128)(2,1)} %pad_maximum_fusion.shard_ref, ...), custom_call_target="tpu_custom_call" | custom-call | tf_op jit(solution)/shard_map/pallas_call | solution.py:595
  230.8 0.8 slice_bitcast_fusion.3
  231.6 1.5 slice_bitcast_fusion.4
  233.1 0.6 copy.28
  233.7 1.5 slice_bitcast_fusion.2
  235.2 0.9 slice.27
  236.1 1.9 slice_bitcast_fusion
  238.0 0.0 copy-start.1
  238.0 0.1 reshape.28
  238.1 0.7 copy.26
  238.8 0.2 copy-done.1
  239.1 0.0 copy-start
  239.1 0.8 copy.31
  239.9 0.4 copy-done
  240.3 0.8 copy.32
  (1 shorter events, 0.0 us)
Async XLA Ops:
  0.6 1.1 copy-start.3
  1.7 0.9 copy-start.2
  1.7 0.9 copy-start.4
  238.0 1.0 copy-start.1
  239.1 1.2 copy-start

commit v2 on v1

v2 whole, which is shorter than its diff:
```python
import functools
import math

import jax
import jax.numpy as jnp
from jax import lax
from jax.experimental import pallas as pl
from jax.experimental.pallas import tpu as pltpu
from jax.sharding import PartitionSpec as P

D = 1024
HD = 64
FF = 4096
SEQ = 256
ROWS = 64
WIDE = 3072
NEGATIVE = -1000000000.0
GELU_COEF = 0.7978845608028654
EPSILON = 1e-05
MESH = pl.DeviceIdType.MESH
BF16 = jnp.bfloat16
F32 = jnp.float32

GAIN, OFFSET, PROJ, QV, FC = 0, 2, 4, 6, 8
SMALL = 16
HALF = ROWS // 2
BOTH = (0, 1)


def scoped(name):
    def deco(func):
        def run(*args, **named):
            with jax.named_scope(name):
                return func(*args, **named)

        return run

    return deco


def dot_nn(a, b):
    return lax.dot_general(a, b, (((1,), (0,)), ((), ())), preferred_element_type=F32)


def dot_nt(a, b):
    return lax.dot_general(a, b, (((1,), (1,)), ((), ())), preferred_element_type=F32)


def dot_tn(a, b):
    return lax.dot_general(a, b, (((0,), (0,)), ((), ())), preferred_element_type=F32)


def norm_rows(hidden, gain_row, offset_row):
    centre = hidden - jnp.mean(hidden, axis=-1, keepdims=True)
    spread = jnp.mean(centre * centre, axis=-1, keepdims=True)
    inverse = lax.rsqrt(spread + EPSILON)
    unit_rows = centre * inverse
    return unit_rows * gain_row + offset_row, unit_rows, inverse


def norm_back(grad_rows, unit_rows, inverse, gain_row):
    grad_unit = grad_rows * gain_row
    return inverse * (
        grad_unit
        - jnp.mean(grad_unit, axis=-1, keepdims=True)
        - unit_rows * jnp.mean(grad_unit * unit_rows, axis=-1, keepdims=True)
    )


def row_sum(value):
    return jnp.sum(value, axis=0, keepdims=True)


def aligned(index, size):
    return pl.ds(pl.multiple_of(index * size, size), size)


def kernel(
    x_ref, cot_ref, seg_ref, qkv_ref, wo_ref, fc1_ref, fc2_ref, gain_ref, offset_ref, qv_ref, proj_ref, fc_ref,
    out_ref, grad_ref, wgrad_ref, late_ref, early_ref,
    w, gd, r0, r1, r2, p1, pb,
    g1, g2, gm, ga, sbuf, rbuf,
    qkv_s, prob_s, mixed_s, active_s, slope_s, unit_s, inv_s, mid_s,
    gb_s, gp_s, gx_s, gt_s, mask_s, dy_s, xs, xr,
    late, early, late_c, late_x, late_y, late_z, early_c, early_x, early_y, early_z,
    z_send, z_recv, gy_send, gy_recv, gx_send, gx_recv, gc_send, gc_recv,
    rc_send, rc_recv, rx_send, rx_recv, ry_send, ry_recv, o_send, o_recv, a_send, a_recv,
):
    s = lax.axis_index("section")
    d = lax.axis_index("dp")
    t = lax.axis_index("tensor")
    x = d // 4
    yl = (d // 2) % 2
    c = d % 2
    y = 2 * s + yl
    mate = {"section": s, "dp": d + 1 - 2 * c, "tensor": t}
    zp = [{"section": s, "dp": d, "tensor": (t + k) % 4} for k in (1, 2, 3)]
    xp = [{"section": s, "dp": ((x + k) % 4) * 4 + yl * 2 + c, "tensor": t} for k in (1, 2, 3)]
    yp = []
    for k in (1, 2, 3):
        other = (y + k) % 4
        yp.append({"section": other // 2, "dp": x * 4 + (other % 2) * 2 + c, "tensor": t})
    across = {"section": 1 - s, "dp": d, "tensor": t}

    def remote(src, dst, send, recv, peer):
        return pltpu.make_async_remote_copy(
            src_ref=src, dst_ref=dst, send_sem=send, recv_sem=recv, device_id=peer, device_id_type=MESH
        )

    pending = {}

    def begin(key, copy, cond=None):
        if cond is None:
            copy.start()
        else:
            pl.when(cond)(copy.start)
        pending.setdefault(key, []).append((copy, cond))

    def flush(key):
        for copy, cond in pending.pop(key, []):
            if cond is None:
                copy.wait_send()
            else:
                pl.when(cond)(copy.wait_send)

    barrier = pltpu.get_barrier_semaphore()
    for peer in zp + xp + yp + [mate]:
        pl.semaphore_signal(barrier, inc=1, device_id=peer, device_id_type=MESH)
    pl.semaphore_wait(barrier, 10)

    def cols(g):
        return pl.ds(g * 1024, 1024)

    def own(g):
        return w.at[s, x, yl, c, :, cols(g)]

    def rows(h):
        return slice(h * HALF, (h + 1) * HALF)

    def part(h):
        return pl.ds(h * HALF, HALF)

    def gather_y(g):
        for k in (1, 2, 3):
            begin("gy", remote(
                own(g), own(g),
                gy_send.at[g, k - 1], gy_recv.at[s, g, k - 1], yp[k - 1],
            ))

    @scoped("gather_x")
    def gather_x(l, g):
        for k in (1, 2, 3):
            src_y = (y - k + 4) % 4
            copy = remote(
                own(g), w.at[l, x, src_y % 2, c, :, cols(g)],
                gy_send.at[g, k - 1], gy_recv.at[l, g, k - 1], yp[k - 1],
            )
            pl.when(src_y // 2 == l)(copy.wait_recv)
        mine = w.at[l, x, :, c, :, cols(g)]
        for k in (1, 2, 3):
            begin("gx", remote(mine, mine, gx_send.at[l, g, k - 1], gx_recv.at[l, g, k - 1], xp[k - 1]))

    @scoped("gather_c")
    def gather_c(l, g):
        for k in (1, 2, 3):
            theirs = w.at[l, (x - k + 4) % 4, :, c, :, cols(g)]
            remote(theirs, theirs, gx_send.at[l, g, k - 1], gx_recv.at[l, g, k - 1], xp[k - 1]).wait_recv()
        half = w.at[l, :, :, c, :, cols(g)]
        begin("gc", remote(half, half, gc_send.at[l, g], gc_recv.at[l, g], mate))

    def turn_x(g):
        for k in (1, 2, 3):
            begin("gx", remote(
                own(g), own(g),
                gx_send.at[0, g, k - 1], gx_recv.at[0, g, k - 1], xp[k - 1],
            ))

    @scoped("turn_y")
    def turn_y(g):
        for k in (1, 2, 3):
            remote(
                own(g), w.at[s, (x - k + 4) % 4, yl, c, :, cols(g)],
                gx_send.at[0, g, k - 1], gx_recv.at[0, g, k - 1], xp[k - 1],
            ).wait_recv()
        mine = w.at[s, :, yl, c, :, cols(g)]
        for k in (1, 2, 3):
            begin("gy", remote(mine, mine, gy_send.at[g, k - 1], gy_recv.at[s, g, k - 1], yp[k - 1]))

    @scoped("turn_c")
    def turn_c(l, g):
        for k in (1, 2, 3):
            src_y = (y - k + 4) % 4
            theirs = w.at[l, :, src_y % 2, c, :, cols(g)]
            copy = remote(theirs, theirs, gy_send.at[g, k - 1], gy_recv.at[l, g, k - 1], yp[k - 1])
            pl.when(src_y // 2 == l)(copy.wait_recv)
        half = w.at[l, :, :, c, :, cols(g)]
        begin("gc", remote(half, half, gc_send.at[l, g], gc_recv.at[l, g], mate))

    @scoped("gather_done")
    def gather_done(l, g):
        half = w.at[l, :, :, 1 - c, :, cols(g)]
        remote(half, half, gc_send.at[l, g], gc_recv.at[l, g], mate).wait_recv()

    def reduce_c(l, g):
        begin(("rc", l, g), remote(
            gd.at[:, :, 1 - c, :, cols(g)], r0.at[l, :, :, :, cols(g)], rc_send.at[l, g], rc_recv.at[l, g], mate
        ))

    @scoped("reduce_x")
    def reduce_x(l, g):
        remote(
            gd.at[:, :, 1 - c, :, cols(g)], r0.at[l, :, :, :, cols(g)], rc_send.at[l, g], rc_recv.at[l, g], mate
        ).wait_recv()

        def add(i, _):
            for half in BOTH:
                gd[i, half, c, :, cols(g)] = (
                    gd[i, half, c, :, cols(g)].astype(F32) + r0[l, i, half, :, cols(g)].astype(F32)
                ).astype(BF16)
            return 0

        lax.fori_loop(0, 4, add, 0)
        for i in range(4):
            begin(("rx", l, g), x_copy(l, g, i))

    def x_copy(l, g, i):
        step, half = ((2, 0), (2, 1), (1, 1), (3, 0), (1, 0), (3, 1))[i]
        return remote(
            gd.at[(x + step) % 4, half, c, :, cols(g)], r1.at[l, i, :, cols(g)],
            rx_send.at[l, g, i], rx_recv.at[l, g, i], xp[2 * (i % 2)],
        )

    @scoped("reduce_f")
    def reduce_f(l, g):
        for i in BOTH:
            x_copy(l, g, i).wait_recv()
            at = (x + 1 + 2 * i) % 4
            gd[at, i, c, :, cols(g)] = (
                gd[at, i, c, :, cols(g)].astype(F32) + r1[l, i, :, cols(g)].astype(F32)
            ).astype(BF16)
            begin(("rx", l, g), x_copy(l, g, 4 + i))

    @scoped("reduce_y")
    def reduce_y(l, g):
        for i in (2, 3, 4, 5):
            x_copy(l, g, i).wait_recv()
        for half in BOTH:
            total = gd[x, half, c, :, cols(g)].astype(F32)
            for i in ((3, 4), (2, 5))[half]:
                total += r1[l, i, :, cols(g)].astype(F32)
            p1[l, half, :, cols(g)] = total.astype(BF16)
        for k in (1, 2, 3):
            target = (y + k) % 4
            begin("ry", remote(
                p1.at[l, target % 2, :, cols(g)], r2.at[l, k - 1, :, cols(g)],
                ry_send.at[l, g, k - 1], ry_recv.at[l, g, k - 1], yp[k - 1],
            ), target // 2 == l)

    @scoped("reduce_done")
    def reduce_done(l, g):
        copies = [
            remote(
                p1.at[l, 0, :, cols(g)], r2.at[l, k, :, cols(g)],
                ry_send.at[l, g, k], ry_recv.at[l, g, k], yp[k],
            )
            for k in (0, 1, 2)
        ]

        @pl.when(s == l)
        def _():
            for copy in copies:
                copy.wait_recv()
            total = p1[l, yl, :, cols(g)].astype(F32)
            for k in (0, 1, 2):
                total += r2[l, k, :, cols(g)].astype(F32)
            wgrad_ref[:, cols(g)] = total

    def spread_start(event, buf, h):
        mine = buf.at[t, part(h)]
        for k in (1, 2, 3):
            begin("z", remote(mine, mine, z_send.at[event, h, k - 1], z_recv.at[event, h, k - 1], zp[k - 1]))

    @scoped("spread_done")
    def spread_done(event, buf, h):
        for k in (1, 2, 3):
            theirs = buf.at[(t - k + 4) % 4, part(h)]
            remote(theirs, theirs, z_send.at[event, h, k - 1], z_recv.at[event, h, k - 1], zp[k - 1]).wait_recv()

    def sum_copy(event, h, k):
        return remote(
            sbuf.at[(event // 2) % 3, (t + k) % 4, part(h)], rbuf.at[event // 2, k - 1, part(h)],
            z_send.at[event, h, k - 1], z_recv.at[event, h, k - 1], zp[k - 1],
        )

    def sum_start(event, h):
        for k in (1, 2, 3):
            begin(("s", (event // 2) % 3, h), sum_copy(event, h, k))

    @scoped("sum_done")
    def sum_done(event, h):
        for k in (1, 2, 3):
            sum_copy(event, h, k).wait_recv()
        total = sbuf[(event // 2) % 3, t, rows(h)].astype(F32)
        for k in (0, 1, 2):
            total += rbuf[event // 2, k, rows(h)].astype(F32)
        return total

    @scoped("share")
    def share(event, h, lhs, l, c0, n):
        slot = (event // 2) % 3
        flush(("s", slot, h))

        def tile(j, _):
            right = w[l, j, :, :, :, pl.ds(c0, n)].reshape(256, n)
            value = dot_nt(lhs().reshape(4 * HALF, n), right).astype(BF16)
            sbuf[slot, :, rows(h), aligned(j, 256)] = value.reshape(4, HALF, 256)
            return 0

        lax.fori_loop(0, 4, tile, 0)
        sum_start(event, h)

    fills = []

    def fill(count):
        for _ in range(min(count, len(fills))):
            fills.pop(0)()

    def weight_grad(lhs_ref, rhs_ref, c0, n, then=None):
        @scoped("weight_grad")
        def one(i):
            left = lhs_ref[:, :, i * 256:(i + 1) * 256].reshape(SEQ, 256).T
            gt_s[...] = left

            def tile(j, _):
                value = dot_nn(gt_s[...], rhs_ref[:, :, aligned(j, 256)].reshape(SEQ, 256))
                gd[i, :, :, :, pl.ds(pl.multiple_of(c0 + j * 256, 256), 256)] = value.astype(
                    BF16
                ).reshape(2, 2, ROWS, 256)
                return 0

            lax.fori_loop(0, n // 256, tile, 0)
            if then is not None and i == 3:
                then()

        for i in range(4):
            fills.append(functools.partial(one, i))

    def cross_send(index, value, l, local_ref, h):
        @pl.when(s == l)
        def _():
            local_ref[s, rows(h)] = value

        @pl.when(s != l)
        def _():
            xs[index, rows(h)] = value

        begin("o", remote(
            xs.at[index, part(h)], xr.at[index, part(h)], o_send.at[index, h], o_recv.at[index, h], across
        ), s != l)

    stages = {
        "c": ((late_c, early_c), c, [mate], 0), "x": ((late_x, early_x), x, xp, 1),
        "y": ((late_y, early_y), y, yp, 4), "z": ((late_z, early_z), t, zp, 7),
    }

    def all_sum(kind, l, stage):
        bufs, _, peers, _ = stages[stage]
        value = bufs[kind][l, 0]
        for k in range(1, len(peers) + 1):
            value = value + bufs[kind][l, k]
        return value

    def all_start(kind, l, stage, before=None):
        bufs, me, peers, at = stages[stage]
        buf = bufs[kind]
        buf[l, me] = (late, early)[kind][l] if before is None else all_sum(kind, l, before)
        for k, peer in enumerate(peers):
            begin("a", remote(
                buf.at[l, me], buf.at[l, me], a_send.at[kind, l, at + k], a_recv.at[kind, l, at + k], peer
            ))

    @scoped("all_wait")
    def all_wait(kind, l, stage):
        bufs, me, peers, at = stages[stage]
        n = len(peers) + 1
        for k, peer in enumerate(peers):
            theirs = bufs[kind].at[l, (me - k - 1 + n) % n]
            remote(theirs, theirs, a_send.at[kind, l, at + k], a_recv.at[kind, l, at + k], peer).wait_recv()

    def all_next(kind, l, stage, following):
        all_wait(kind, l, stage)
        all_start(kind, l, following, stage)

    def small(l, row):
        return pb[l, row:row + 1]

    def norm_one(l, h, hidden):
        normed, unit, inverse = norm_rows(hidden, small(l, GAIN), small(l, OFFSET))
        unit_s[l, 0, rows(h)] = unit
        inv_s[l, 0, rows(h)] = inverse
        g1[l, t, rows(h)] = normed.astype(BF16)
        spread_start(4 * l, g1.at[l], h)
        mid_s[rows(h)] = hidden

    def project(l, h):
        left = g1[l, :, rows(h)].reshape(4 * HALF, D)
        for j in range(3):
            value = dot_nn(left, w[l, :, :, :, :, j * 256:(j + 1) * 256].reshape(D, 256))
            if j != 1:
                value = value + pb[l, QV + j // 2:QV + j // 2 + 1, aligned(t, 256)]
            qkv_s[l, :, rows(h), j * 256:(j + 1) * 256] = value.astype(BF16).reshape(4, HALF, 256)

    def head(l, j, n):
        return qkv_s[l, :, :, j * 256 + n * HD:j * 256 + (n + 1) * HD].reshape(SEQ, HD)

    @scoped("attend")
    def attend(l):
        for pair in range(2):
            mixed = []
            for n in (2 * pair, 2 * pair + 1):
                scores = dot_nt(head(l, 0, n), head(l, 1, n)) * 0.125
                scores = jnp.where(mask_s[...] > 0.5, scores, NEGATIVE)
                shifted = jnp.exp(scores - jnp.max(scores, axis=-1, keepdims=True))
                probs = shifted / jnp.sum(shifted, axis=-1, keepdims=True)
                prob_s[l, n] = probs
                mixed.append(dot_nn(probs.astype(BF16), head(l, 2, n)))
            both = jnp.concatenate(mixed, axis=1).astype(BF16)
            mixed_s[l, :, :, pair * 128:(pair + 1) * 128] = both.reshape(4, ROWS, 128)

    def norm_two(l, h):
        middle = mid_s[rows(h)] + (sum_done(4 * l + 1, h) + small(l, PROJ))
        normed, unit, inverse = norm_rows(middle, small(l, GAIN + 1), small(l, OFFSET + 1))
        unit_s[l, 1, rows(h)] = unit
        inv_s[l, 1, rows(h)] = inverse
        g2[l, t, rows(h)] = normed.astype(BF16)
        spread_start(4 * l + 2, g2.at[l], h)
        mid_s[rows(h)] = middle

    @scoped("up")
    def up(l, h):
        def tile(j, _):
            at = aligned(j, 256)
            before = dot_nn(
                g2[l, :, rows(h)].reshape(4 * HALF, D),
                w[l, :, :, :, :, pl.ds(pl.multiple_of(1024 + j * 256, 256), 256)].reshape(D, 256),
            ) + pb[l, pl.ds(FC + t, 1), at]
            tanh_part = jnp.tanh(GELU_COEF * (before + 0.044715 * before * before * before))
            active = (0.5 * before * (1.0 + tanh_part)).astype(BF16)
            slope = 0.5 * (1.0 + tanh_part) + 0.5 * before * (
                1.0 - tanh_part * tanh_part
            ) * GELU_COEF * (1.0 + 3.0 * 0.044715 * before * before)
            active_s[l, :, rows(h), at] = active.reshape(4, HALF, 256)
            if l == 0:
                slope_s[l, :, rows(h), at] = slope.reshape(4, HALF, 256)
            else:
                grad_before = slope_s[l, :, rows(h), at].reshape(4 * HALF, 256) * slope
                early[l, pl.ds(4 + t, 1), at] += row_sum(grad_before)
                gb_s[:, rows(h), at] = grad_before.astype(BF16).reshape(4, HALF, 256)
            return 0

        lax.fori_loop(0, 4, tile, 0)

    def layer_out(l, h):
        return mid_s[rows(h)] + (sum_done(4 * l + 3, h) + small(l, PROJ + 1))

    def attention_part(l):
        for h in BOTH:
            spread_done(4 * l, g1.at[l], h)
            if h == 0:
                gather_done(l, 0)
            project(l, h)
        attend(l)
        for h in BOTH:
            share(4 * l + 1, h, lambda h=h: mixed_s[l, :, rows(h)], l, 768, 256)

    @scoped("before_up")
    def before_up(l):
        def tile(j, _):
            value = dot_nn(
                gm[l].reshape(SEQ, D),
                w[l, :, :, :, :, pl.ds(pl.multiple_of(2048 + j * 256, 256), 256)].reshape(D, 256),
            )
            slope_s[l, :, :, aligned(j, 256)] = value.reshape(4, ROWS, 256)
            return 0

        lax.fori_loop(0, 4, tile, 0)

    @scoped("down")
    def down(l, h):
        def tile(j, _):
            at = aligned(j, 256)
            grad_before = dot_nn(
                gm[l, :, rows(h)].reshape(4 * HALF, D),
                w[l, :, :, :, :, pl.ds(pl.multiple_of(2048 + j * 256, 256), 256)].reshape(D, 256),
            ) * slope_s[l, :, rows(h), at].reshape(4 * HALF, 256)
            early[l, pl.ds(4 + t, 1), at] += row_sum(grad_before)
            gb_s[:, rows(h), at] = grad_before.astype(BF16).reshape(4, HALF, 256)
            return 0

        lax.fori_loop(0, 4, tile, 0)

    def norm_two_back(l, h):
        grad = sum_done(13 - 4 * l, h)
        unit = unit_s[l, 1, rows(h)]
        early[l, 0:1] += row_sum(grad * unit)
        early[l, 1:2] += row_sum(grad)
        grad_middle = dy_s[rows(h)] + norm_back(grad, unit, inv_s[l, 1, rows(h)], small(l, GAIN + 1))
        dy_s[rows(h)] = grad_middle
        ga[l, t, rows(h)] = grad_middle.astype(BF16)
        spread_start(14 - 4 * l, ga.at[l], h)
        early[l, 2:3] += row_sum(grad_middle)

    def mixed_back(l, h):
        value = dot_nn(
            ga[l, :, rows(h)].reshape(4 * HALF, D), w[l, :, :, :, :, 768:1024].reshape(D, 256)
        )
        gx_s[:, rows(h)] = value.astype(BF16).reshape(4, HALF, 256)

    @scoped("attend_back")
    def attend_back(l):
        for pair in range(2):
            grads = [[], [], []]
            for n in (2 * pair, 2 * pair + 1):
                q, key, value = head(l, 0, n), head(l, 1, n), head(l, 2, n)
                grad_head = gx_s[:, :, n * HD:(n + 1) * HD].reshape(SEQ, HD)
                probs = prob_s[l, n]
                grad_probs = dot_nt(grad_head, value)
                row_dot = jnp.sum(probs * grad_probs, axis=-1, keepdims=True)
                grad_scores = (probs * (grad_probs - row_dot)).astype(BF16)
                grads[0].append(dot_nn(grad_scores, key) * 0.125)
                grads[1].append(dot_tn(grad_scores, q) * 0.125)
                grads[2].append(dot_tn(probs.astype(BF16), grad_head))
            for j in range(3):
                both = jnp.concatenate(grads[j], axis=1)
                gp_s[:, :, j * 256 + pair * 128:j * 256 + (pair + 1) * 128] = both.astype(BF16).reshape(
                    4, ROWS, 128
                )
                if j != 1:
                    total = row_sum(both)
                    for k in BOTH:
                        late[l, 4 + j + k:5 + j + k, aligned((t % 2) * 2 + pair, 128)] = jnp.where(
                            t // 2 == k, total, 0.0
                        )

    def norm_one_back(l, h):
        grad = sum_done(15 - 4 * l, h)
        unit = unit_s[l, 0, rows(h)]
        for row, value in ((0, row_sum(grad * unit)), (2, row_sum(grad))):
            late[l, row:row + 1] += value[:, :512]
            late[l, row + 1:row + 2] += value[:, 512:]
        return dy_s[rows(h)] + norm_back(grad, unit, inv_s[l, 0, rows(h)], small(l, GAIN))

    pb[s, GAIN:GAIN + 2] = gain_ref[...]
    pb[s, OFFSET:OFFSET + 2] = offset_ref[...]
    pb[s, PROJ:PROJ + 2] = proj_ref[...]
    pb[s, QV:QV + 2] = qv_ref[...]
    for k in range(4):
        pb[s, FC + k:FC + k + 1] = fc_ref[:, k * 1024:(k + 1) * 1024]
    pb[s, FC + 4:] = jnp.zeros((SMALL - FC - 4, D), F32)
    begin("pb", remote(pb.at[s], pb.at[s], o_send.at[2, 0], o_recv.at[2, 0], across))
    for j in range(3):
        w[s, x, yl, c, :, j * 256:(j + 1) * 256] = qkv_ref[j]
    w[s, x, yl, c, :, 768:1024] = wo_ref[...]
    gather_y(0)
    w[s, x, yl, c, :, 2048:] = fc2_ref[...]
    turn_x(2)
    w[s, x, yl, c, :, 1024:2048] = fc1_ref[...]
    late[...] = jnp.zeros_like(late)
    early[...] = jnp.zeros_like(early)
    seg_rows = jnp.broadcast_to(seg_ref[s].astype(F32), (SEQ, SEQ))
    seg_cols = seg_rows.T
    places_i = lax.broadcasted_iota(jnp.int32, (SEQ, SEQ), 0)
    places_j = lax.broadcasted_iota(jnp.int32, (SEQ, SEQ), 1)
    mask_s[...] = jnp.where((seg_rows == seg_cols) & (places_i >= places_j), 1.0, 0.0)
    with jax.named_scope("wait_pb"):
        remote(pb.at[1 - s], pb.at[1 - s], o_send.at[2, 0], o_recv.at[2, 0], across).wait_recv()
    for h in BOTH:
        norm_one(0, h, x_ref[s, rows(h)].astype(F32))
    gather_x(0, 0)
    gather_y(1)
    turn_y(2)
    gm[1, t] = cot_ref[s]
    for h in BOTH:
        spread_start(8, gm.at[1], h)
    dy_s[...] = cot_ref[s].astype(F32)
    early[1, 3:4] = row_sum(dy_s[...])
    gather_c(0, 0)
    gather_x(0, 1)

    attention_part(0)
    for h in BOTH:
        norm_two(0, h)
    gather_c(0, 1)
    gather_x(1, 0)
    for h in BOTH:
        spread_done(2, g2.at[0], h)
        if h == 0:
            gather_done(0, 1)
        up(0, h)
        if h == 0:
            turn_c(0, 2)
            gather_done(0, 2)
        share(3, h, lambda h=h: active_s[0, :, rows(h)], 0, 2048, 1024)
    turn_c(1, 2)
    gather_c(1, 0)
    gather_x(1, 1)
    for h in BOTH:
        hidden = layer_out(0, h)
        norm_one(1, h, hidden.astype(BF16).astype(F32))
        cross_send(0, hidden, 0, out_ref, h)

    attention_part(1)
    gather_done(1, 2)
    for h in BOTH:
        spread_done(8, gm.at[1], h)
    before_up(1)
    for h in BOTH:
        norm_two(1, h)
    gather_c(1, 1)
    weight_grad(gm.at[1], active_s.at[1], 2048, 1024, lambda: reduce_c(1, 2))
    weight_grad(g2.at[1], gb_s, 1024, 1024, lambda: reduce_c(1, 1))
    for h in BOTH:
        spread_done(6, g2.at[1], h)
        if h == 0:
            gather_done(1, 1)
        up(1, h)
        share(9, h, lambda h=h: gb_s[:, rows(h)], 1, 1024, 1024)
    fill(4)
    norm_two_back(1, 0)
    fill(2)
    norm_two_back(1, 1)
    fill(1)
    reduce_x(1, 2)
    fill(1)
    share(7, 0, lambda: active_s[1, :, rows(0)], 1, 2048, 1024)
    spread_done(10, ga.at[1], 0)
    mixed_back(1, 0)
    share(7, 1, lambda: active_s[1, :, rows(1)], 1, 2048, 1024)
    spread_done(10, ga.at[1], 1)
    mixed_back(1, 1)
    reduce_x(1, 1)
    attend_back(1)
    for h in BOTH:
        share(11, h, lambda h=h: gp_s[:, rows(h)], 1, 0, 768)
    reduce_f(1, 2)
    weight_grad(ga.at[1], mixed_s.at[1], 768, 256)
    weight_grad(g1.at[1], gp_s, 0, 768, lambda: reduce_c(1, 0))
    fill(8)

    def pass_grad(h):
        grad = norm_one_back(1, h).astype(BF16)
        gm[0, t, rows(h)] = grad
        spread_start(12, gm.at[0], h)
        dy_s[rows(h)] = grad.astype(F32)
        cross_send(3, grad.astype(F32), 1, grad_ref, h)

    pass_grad(0)
    reduce_f(1, 1)
    for h in BOTH:
        hidden = layer_out(1, h)
        cross_send(2, hidden, 1, out_ref, h)
    pass_grad(1)
    reduce_x(1, 0)
    reduce_y(1, 2)
    early[0, 3:4] = row_sum(dy_s[...])
    for kind in BOTH:
        all_start(kind, 1, "c")
    flush(("rc", 1, 2))
    flush(("rx", 1, 2))

    for h in BOTH:
        spread_done(12, gm.at[0], h)
        down(0, h)
        share(13, h, lambda h=h: gb_s[:, rows(h)], 0, 1024, 1024)
    reduce_f(1, 0)
    weight_grad(gm.at[0], active_s.at[0], 2048, 1024, lambda: reduce_c(0, 2))
    weight_grad(g2.at[0], gb_s, 1024, 1024, lambda: reduce_c(0, 1))
    fill(4)
    norm_two_back(0, 0)
    reduce_y(1, 1)
    flush(("rc", 1, 1))
    flush(("rx", 1, 1))
    fill(2)
    norm_two_back(0, 1)
    reduce_x(0, 2)
    fill(2)
    for kind in BOTH:
        all_next(kind, 1, "c", "y")
    spread_done(14, ga.at[0], 0)
    mixed_back(0, 0)
    reduce_y(1, 0)
    flush(("rc", 1, 0))
    flush(("rx", 1, 0))
    spread_done(14, ga.at[0], 1)
    mixed_back(0, 1)
    reduce_x(0, 1)
    attend_back(0)
    for h in BOTH:
        share(15, h, lambda h=h: gp_s[:, rows(h)], 0, 0, 768)
    reduce_f(0, 2)
    all_start(1, 0, "c")
    weight_grad(ga.at[0], mixed_s.at[0], 768, 256)
    weight_grad(g1.at[0], gp_s, 0, 768, lambda: reduce_c(0, 0))
    fill(8)
    cross_send(1, norm_one_back(0, 0), 0, grad_ref, 0)
    reduce_f(0, 1)
    all_next(1, 0, "c", "y")
    for kind in BOTH:
        all_next(kind, 1, "y", "x")
    cross_send(1, norm_one_back(0, 1), 0, grad_ref, 1)
    all_start(0, 0, "c")
    reduce_x(0, 0)
    all_next(0, 0, "c", "z")
    reduce_y(0, 2)
    for kind in BOTH:
        all_next(kind, 1, "x", "z")
    all_next(1, 0, "y", "x")
    reduce_y(0, 1)
    all_next(0, 0, "z", "y")
    reduce_f(0, 0)
    all_next(0, 0, "y", "x")
    all_next(1, 0, "x", "z")
    for g in (2, 1, 0):
        reduce_done(1, g)
    for kind in BOTH:
        all_wait(kind, 1, "z")
    reduce_y(0, 0)
    all_wait(0, 0, "x")
    all_wait(1, 0, "z")
    for kind, ref in ((0, late_ref), (1, early_ref)):
        ref[...] = jnp.where(s == 0, all_sum(kind, 0, "zx"[1 - kind]), all_sum(kind, 1, "z"))
    for ref, pairs in ((out_ref, (0, 2)), (grad_ref, (1, 3))):
        for h in BOTH:
            first, second = [
                remote(
                    xs.at[index, part(h)], xr.at[index, part(h)], o_send.at[index, h], o_recv.at[index, h], across
                )
                for index in pairs
            ]
            pl.when(s == 0)(first.wait_recv)
            pl.when(s == 1)(second.wait_recv)

        @pl.when(s == 0)
        def _():
            ref[1 - s] = xr[pairs[0]]

        @pl.when(s == 1)
        def _():
            ref[1 - s] = xr[pairs[1]]

    for g in (2, 1, 0):
        reduce_done(0, g)
    for key in list(pending):
        flush(key)


def finish(
    out_ref, grad_ref, wgrad_ref, late_ref, early_ref,
    outs, grads, qkv, out, fc1, fc2, gain, offset, qv, proj, fc,
):
    outs[0] = out_ref[...]
    grads[0] = grad_ref[...]
    for j in range(3):
        qkv[0, j] = wgrad_ref[:, j * 256:(j + 1) * 256]
    out[0] = wgrad_ref[:, 768:1024]
    fc1[0] = wgrad_ref[:, 1024:2048]
    fc2[0] = wgrad_ref[:, 2048:]
    for ref, row, other in ((gain, 0, 0), (offset, 2, 1)):
        for k in BOTH:
            ref[0, 0:1, k * 512:(k + 1) * 512] = late_ref[row + k:row + k + 1]
        ref[0, 1:2] = early_ref[other:other + 1]
    for row in BOTH:
        for k in BOTH:
            at = 4 + 2 * row + k
            qv[0, row:row + 1, k * 512:(k + 1) * 512] = late_ref[at:at + 1]
    proj[0] = early_ref[2:4]
    for k in range(4):
        fc[:, k * 1024:(k + 1) * 1024] = early_ref[4 + k:5 + k]


def fused(*args):
    vmem = pl.BlockSpec(memory_space=pltpu.VMEM)
    dma = pltpu.SemaphoreType.DMA
    scratch = [
        pltpu.VMEM((2, 4, 2, 2, ROWS, WIDE), BF16),
        pltpu.VMEM((4, 2, 2, ROWS, WIDE), BF16),
        pltpu.VMEM((2, 4, 2, ROWS, WIDE), BF16),
        pltpu.VMEM((2, 6, ROWS, WIDE), BF16),
        pltpu.VMEM((2, 3, ROWS, WIDE), BF16),
        pltpu.VMEM((2, 2, ROWS, WIDE), BF16),
        pltpu.VMEM((2, SMALL, D), F32),
        pltpu.VMEM((2, 4, ROWS, D), BF16),
        pltpu.VMEM((2, 4, ROWS, D), BF16),
        pltpu.VMEM((2, 4, ROWS, D), BF16),
        pltpu.VMEM((2, 4, ROWS, D), BF16),
        pltpu.VMEM((3, 4, ROWS, D), BF16),
        pltpu.VMEM((8, 3, ROWS, D), BF16),
        pltpu.VMEM((2, 4, ROWS, 768), BF16),
        pltpu.VMEM((2, 4, SEQ, SEQ), F32),
        pltpu.VMEM((2, 4, ROWS, 256), BF16),
        pltpu.VMEM((2, 4, ROWS, D), BF16),
        pltpu.VMEM((2, 4, ROWS, D), F32),
        pltpu.VMEM((2, 2, ROWS, D), F32),
        pltpu.VMEM((2, 2, ROWS, 1), F32),
        pltpu.VMEM((ROWS, D), F32),
        pltpu.VMEM((4, ROWS, D), BF16),
        pltpu.VMEM((4, ROWS, 768), BF16),
        pltpu.VMEM((4, ROWS, 256), BF16),
        pltpu.VMEM((256, SEQ), BF16),
        pltpu.VMEM((SEQ, SEQ), F32),
        pltpu.VMEM((ROWS, D), F32),
        pltpu.VMEM((4, ROWS, D), F32),
        pltpu.VMEM((4, ROWS, D), F32),
        pltpu.VMEM((2, 8, 512), F32),
        pltpu.VMEM((2, 8, D), F32),
    ]
    for width in (512, D):
        scratch += [pltpu.VMEM((2, n, 8, width), F32) for n in (2, 4, 4, 4)]
    scratch += [
        dma((16, 2, 3)), dma((16, 2, 3)),
        dma((3, 3)), dma((2, 3, 3)),
        dma((2, 3, 3)), dma((2, 3, 3)),
        dma((2, 3)), dma((2, 3)),
        dma((2, 3)), dma((2, 3)),
        dma((2, 3, 6)), dma((2, 3, 6)),
        dma((2, 3, 3)), dma((2, 3, 3)),
        dma((4, 2)), dma((4, 2)),
        dma((2, 2, 10)), dma((2, 2, 10)),
    ]
    sums = pl.pallas_call(
        kernel,
        out_shape=(
            jax.ShapeDtypeStruct((2, ROWS, D), F32),
            jax.ShapeDtypeStruct((2, ROWS, D), F32),
            jax.ShapeDtypeStruct((ROWS, WIDE), F32),
            jax.ShapeDtypeStruct((8, 512), F32),
            jax.ShapeDtypeStruct((8, D), F32),
        ),
        in_specs=[vmem] * 12,
        out_specs=(vmem,) * 5,
        scratch_shapes=scratch,
        compiler_params=pltpu.CompilerParams(
            collective_id=0, has_side_effects=True, vmem_limit_bytes=62 * 2**20
        ),
    )(*args)
    return pl.pallas_call(
        finish,
        out_shape=(
            jax.ShapeDtypeStruct((1, 2, ROWS, D), F32),
            jax.ShapeDtypeStruct((1, 2, ROWS, D), F32),
            jax.ShapeDtypeStruct((1, 3, ROWS, 256), F32),
            jax.ShapeDtypeStruct((1, ROWS, 256), F32),
            jax.ShapeDtypeStruct((1, ROWS, 1024), F32),
            jax.ShapeDtypeStruct((1, ROWS, 1024), F32),
            jax.ShapeDtypeStruct((1, 2, D), F32),
            jax.ShapeDtypeStruct((1, 2, D), F32),
            jax.ShapeDtypeStruct((1, 2, D), F32),
            jax.ShapeDtypeStruct((1, 2, D), F32),
            jax.ShapeDtypeStruct((1, FF), F32),
        ),
        in_specs=[vmem] * 5,
        out_specs=(vmem,) * 11,
    )(*sums)


def local(
    inputs, cotangent, segments, qkv_weight, out_weight, fc1_weight, fc2_weight,
    ln_gains, ln_biases, qv_bias, proj_biases, fc_bias,
):
    outs, grads, qkv, out, fc1, fc2, gain, offset, qv, proj, fc = fused(
        inputs, cotangent, segments,
        jnp.transpose(qkv_weight[0], (1, 0, 2)), out_weight[0].T, fc1_weight[0], fc2_weight[0].T,
        ln_gains[0], ln_biases[0], qv_bias[0], proj_biases[0], fc_bias,
    )
    return (
        outs, grads, jnp.transpose(qkv, (0, 2, 1, 3)), jnp.transpose(out, (0, 2, 1)), fc1,
        jnp.transpose(fc2, (0, 2, 1)), gain, offset, qv, proj, fc,
    )


def solution(mesh):
    in_specs = (
        P(None, ("dp", "tensor"), None),
        P(None, ("dp", "tensor"), None),
        P(None, "dp", None),
        P("section", "dp", None, "tensor"),
        P("section", "tensor", "dp"),
        P("section", "dp", "tensor"),
        P("section", "tensor", "dp"),
        P("section", None, None),
        P("section", None, None),
        P("section", None, None),
        P("section", None, None),
        P("section", None),
    )
    out_specs = (
        P("section", None, ("dp", "tensor"), None),
        P("section", None, ("dp", "tensor"), None),
        P("section", "dp", None, "tensor"),
        P("section", "tensor", "dp"),
        P("section", "dp", "tensor"),
        P("section", "tensor", "dp"),
        P("section", None, None),
        P("section", None, None),
        P("section", None, None),
        P("section", None, None),
        P("section", None),
    )
    return jax.shard_map(local, mesh=mesh, in_specs=in_specs, out_specs=out_specs, check_vma=False)
```

time: 243 us -> 176 us (0.72)
  Pallas kernels: 227 us -> 175 us
  local copies, waits for them, and re-layouts: 12.1 us -> 0 us
    pallas_call x1, Pallas kernels: 227 us -> 172 us  [fused(): pl.pallas_call(kernel, out_shape=(jax.ShapeDtypeStruct((2, ROWS, D), F32)...]
    unnamed x17 -> x0, local copies, waits for them, and re-layouts: 6.23 us -> none
    broadcast_in_dim x3 -> x0, local copies, waits for them, and re-layouts: 4.86 us -> none  [the longest x1 1.87 us: local(): wgrad[:, 2048:].T[None]]
    pallas_call x0 -> x1, Pallas kernels: none -> 2.74 us  [fused(): pl.pallas_call(finish, out_shape=(jax.ShapeDtypeStruct((1, 2, ROWS, D), F...]
where the time goes in v2:
time: 176 us
  Pallas kernels  175 us (99%)
    pallas_call x1, Pallas kernels, fused(): pl.pallas_call(kernel, out_shape=(jax.ShapeDtypeStruct((2, ROWS, D), F32)...  172 us

profile of v2, /device:TPU:0, one launch (start us, length us, event | category | flops | bytes accessed | tf_op | source)
XLA Modules:
  0.0 175.9 jit_solution(5718955065110041001)
XLA Ops:
  0.6 172.4 %shard_map.203 = (f32[2,64,1024]{2,1,0:T(8,128)}, f32[2,64,1024]{2,1,0:T(8,128)}, f32[64,3072]{1,0:T(8,128)}, f32[8,512]{1,0:T(8,128)}, f32[8,1024]{1,0:T(8,128)}) custom-call(bf16[2,64,1024]{2,1,0:T(8,128)(2,1)} %x_ref.1, bf16[2,64,1024]{2,1,0:T(8,128)(2,1)} %cot_ref.1, s32[2,1,256]{2,1,0:T(1,128)} %seg_ref.1, bf16[3,64,256]{2,1,0:T(8,128)(2,1)} %bitcast.19, ...), custom_call_target="tpu_custom_call" | custom-call | tf_op jit(solution)/shard_map/pallas_call | solution.py:830
  173.1 2.7 %shard_map.204 = (f32[1,2,64,1024]{3,2,1,0:T(8,128)}, f32[1,2,64,1024]{3,2,1,0:T(8,128)}, f32[1,3,64,256]{3,2,1,0:T(8,128)}, f32[1,64,256]{2,1,0:T(8,128)}, f32[...) custom-call(f32[2,64,1024]{2,1,0:T(8,128)} %get-tuple-element.27.out, ...), custom_call_target="tpu_custom_call" | custom-call | tf_op jit(solution)/shard_map/pallas_call | solution.py:846

commit v3 on v2

--- a/solution.py
+++ b/solution.py
@@ -25,6 +25,8 @@
 SMALL = 16
 HALF = ROWS // 2
 BOTH = (0, 1)
+GATHER = ((0, 768), (768, 256), (1024, 512), (1536, 512), (2048, 256), (2304, 768))
+REDUCE = ((0, 768), (768, 256), (1024, 1024), (2048, 512), (2560, 512))
 
 
 def scoped(name):
@@ -78,7 +80,7 @@
 def kernel(
     x_ref, cot_ref, seg_ref, qkv_ref, wo_ref, fc1_ref, fc2_ref, gain_ref, offset_ref, qv_ref, proj_ref, fc_ref,
     out_ref, grad_ref, wgrad_ref, late_ref, early_ref,
-    w, gd, r0, r1, r2, p1, pb,
+    w, gd, r0, r1, r2, rq, p1, pb,
     g1, g2, gm, ga, sbuf, rbuf,
     qkv_s, prob_s, mixed_s, active_s, slope_s, unit_s, inv_s, mid_s,
     gb_s, gp_s, gx_s, gt_s, mask_s, dy_s, xs, xr,
@@ -100,6 +102,8 @@
     for k in (1, 2, 3):
         other = (y + k) % 4
         yp.append({"section": other // 2, "dp": x * 4 + (other % 2) * 2 + c, "tensor": t})
+    pair = {"section": s, "dp": x * 4 + (1 - yl) * 2 + c, "tensor": t}
+    beyond = {"section": 1 - s, "dp": x * 4 + (1 - yl) * 2 + c, "tensor": t}
     across = {"section": 1 - s, "dp": d, "tensor": t}
 
     def remote(src, dst, send, recv, peer):
@@ -129,7 +133,13 @@
     pl.semaphore_wait(barrier, 10)
 
     def cols(g):
-        return pl.ds(g * 1024, 1024)
+        return pl.ds(*GATHER[g])
+
+    def near(g):
+        return pl.ds(REDUCE[g][0] - 2560, REDUCE[g][1])
+
+    def wcols(g):
+        return pl.ds(*REDUCE[g])
 
     def own(g):
         return w.at[s, x, yl, c, :, cols(g)]
@@ -201,32 +211,32 @@
         half = w.at[l, :, :, 1 - c, :, cols(g)]
         remote(half, half, gc_send.at[l, g], gc_recv.at[l, g], mate).wait_recv()
 
-    def reduce_c(l, g):
-        begin(("rc", l, g), remote(
-            gd.at[:, :, 1 - c, :, cols(g)], r0.at[l, :, :, :, cols(g)], rc_send.at[l, g], rc_recv.at[l, g], mate
-        ))
-
-    @scoped("reduce_x")
-    def reduce_x(l, g):
-        remote(
-            gd.at[:, :, 1 - c, :, cols(g)], r0.at[l, :, :, :, cols(g)], rc_send.at[l, g], rc_recv.at[l, g], mate
-        ).wait_recv()
-
-        def add(i, _):
-            for half in BOTH:
-                gd[i, half, c, :, cols(g)] = (
-                    gd[i, half, c, :, cols(g)].astype(F32) + r0[l, i, half, :, cols(g)].astype(F32)
-                ).astype(BF16)
-            return 0
-
-        lax.fori_loop(0, 4, add, 0)
-        for i in range(4):
+    def c_copy(l, g, step):
+        at = (x + step) % 4
+        return remote(
+            gd.at[at, :, 1 - c, :, wcols(g)], r0.at[l, at, :, :, wcols(g)],
+            rc_send.at[l, g, step], rc_recv.at[l, g, step], mate,
+        )
+
+    @scoped("reduce_c")
+    def reduce_c(l, g, step):
+        c_copy(l, g, step).wait_recv()
+        at = (x + step) % 4
+        for half in BOTH:
+            gd[at, half, c, :, wcols(g)] = (
+                gd[at, half, c, :, wcols(g)].astype(F32) + r0[l, at, half, :, wcols(g)].astype(F32)
+            ).astype(BF16)
+        if y_first(l, g):
+            if step == 0:
+                begin(("rx", l, g), wide_pair(l, g))
+            return
+        for i in {2: (0, 1), 1: (2,), 3: (3,), 0: ()}[step]:
             begin(("rx", l, g), x_copy(l, g, i))
 
     def x_copy(l, g, i):
         step, half = ((2, 0), (2, 1), (1, 1), (3, 0), (1, 0), (3, 1))[i]
         return remote(
-            gd.at[(x + step) % 4, half, c, :, cols(g)], r1.at[l, i, :, cols(g)],
+            gd.at[(x + step) % 4, half, c, :, wcols(g)], r1.at[l, i, :, wcols(g)],
             rx_send.at[l, g, i], rx_recv.at[l, g, i], xp[2 * (i % 2)],
         )
 
@@ -235,8 +245,8 @@
         for i in BOTH:
             x_copy(l, g, i).wait_recv()
             at = (x + 1 + 2 * i) % 4
-            gd[at, i, c, :, cols(g)] = (
-                gd[at, i, c, :, cols(g)].astype(F32) + r1[l, i, :, cols(g)].astype(F32)
+            gd[at, i, c, :, wcols(g)] = (
+                gd[at, i, c, :, wcols(g)].astype(F32) + r1[l, i, :, wcols(g)].astype(F32)
             ).astype(BF16)
             begin(("rx", l, g), x_copy(l, g, 4 + i))
 
@@ -245,35 +255,135 @@
         for i in (2, 3, 4, 5):
             x_copy(l, g, i).wait_recv()
         for half in BOTH:
-            total = gd[x, half, c, :, cols(g)].astype(F32)
+            total = gd[x, half, c, :, wcols(g)].astype(F32)
             for i in ((3, 4), (2, 5))[half]:
-                total += r1[l, i, :, cols(g)].astype(F32)
-            p1[l, half, :, cols(g)] = total.astype(BF16)
-        for k in (1, 2, 3):
-            target = (y + k) % 4
-            begin("ry", remote(
-                p1.at[l, target % 2, :, cols(g)], r2.at[l, k - 1, :, cols(g)],
-                ry_send.at[l, g, k - 1], ry_recv.at[l, g, k - 1], yp[k - 1],
-            ), target // 2 == l)
+                total += r1[l, i, :, wcols(g)].astype(F32)
+            p1[l, half, :, wcols(g)] = total.astype(BF16)
+        if direct(l, g):
+            for k in (1, 2, 3):
+                target = (y + k) % 4
+                begin("ry", remote(
+                    p1.at[l, target % 2, :, wcols(g)], r2.at[l, k - 1, :, wcols(g)],
+                    ry_send.at[l, g, k - 1], ry_recv.at[l, g, k - 1], yp[k - 1],
+                ), target // 2 == l)
+        else:
+            begin("ry", pair_copy(l, g))
+
+    def y_first(l, g):
+        return l == 0 and g > 3
+
+    def wide_pair(l, g):
+        return remote(
+            gd.at[:, (s + l + 1 + yl) % 2, c, :, wcols(g)], rq.at[0, :, :, near(g)],
+            rx_send.at[l, g, 0], rx_recv.at[l, g, 0], pair,
+        )
+
+    def wide_cut(l, g):
+        return remote(
+            gd.at[:, 1 - yl, c, :, wcols(g)], rq.at[1, :, :, near(g)],
+            rx_send.at[l, g, 1], rx_recv.at[l, g, 1], beyond,
+        )
+
+    def last_x(l, g, k):
+        return remote(
+            gd.at[(x + k) % 4, yl, c, :, wcols(g)], r1.at[l, k - 1, :, wcols(g)],
+            rx_send.at[l, g, k + 1], rx_recv.at[l, g, k + 1], xp[k - 1],
+        )
+
+    @scoped("wide_y")
+    def wide_y(l, g):
+        @pl.when(s != l)
+        def _():
+            wide_pair(l, g).wait_recv()
+
+            def add(i, _):
+                gd[i, 1 - yl, c, :, wcols(g)] = (
+                    gd[i, 1 - yl, c, :, wcols(g)].astype(F32) + rq[0, i, :, near(g)].astype(F32)
+                ).astype(BF16)
+                return 0
+
+            lax.fori_loop(0, 4, add, 0)
+
+        begin(("rx", l, g), wide_cut(l, g), s != l)
+
+    @scoped("wide_x")
+    def wide_x(l, g):
+        @pl.when(s == l)
+        def _():
+            wide_pair(l, g).wait_recv()
+            wide_cut(l, g).wait_recv()
+
+            def add(i, _):
+                gd[i, yl, c, :, wcols(g)] = (
+                    gd[i, yl, c, :, wcols(g)].astype(F32)
+                    + rq[0, i, :, near(g)].astype(F32)
+                    + rq[1, i, :, near(g)].astype(F32)
+                ).astype(BF16)
+                return 0
+
+            lax.fori_loop(0, 4, add, 0)
+
+        for k in (1, 2, 3):
+            begin(("rx", l, g), last_x(l, g, k), s == l)
+
+    @scoped("wide_done")
+    def wide_done(l, g):
+        @pl.when(s == l)
+        def _():
+            for k in (1, 2, 3):
+                last_x(l, g, k).wait_recv()
+            total = gd[x, yl, c, :, wcols(g)].astype(F32)
+            for k in (0, 1, 2):
+                total += r1[l, k, :, wcols(g)].astype(F32)
+            wgrad_ref[:, wcols(g)] = total
+
+    def direct(l, g):
+        return l == 0 and g < 2
+
+    def pair_copy(l, g):
+        return remote(
+            p1.at[l, (s + l + 1 + yl) % 2, :, wcols(g)], r2.at[l, 0, :, wcols(g)],
+            ry_send.at[l, g, 0], ry_recv.at[l, g, 0], pair,
+        )
+
+    def cut_copy(l, g):
+        return remote(
+            p1.at[l, 1 - yl, :, wcols(g)], r2.at[l, 1, :, wcols(g)],
+            ry_send.at[l, g, 1], ry_recv.at[l, g, 1], beyond,
+        )
+
+    @scoped("reduce_g")
+    def reduce_g(l, g):
+        @pl.when(s != l)
+        def _():
+            pair_copy(l, g).wait_recv()
+            p1[l, 1 - yl, :, wcols(g)] = (
+                p1[l, 1 - yl, :, wcols(g)].astype(F32) + r2[l, 0, :, wcols(g)].astype(F32)
+            ).astype(BF16)
+
+        begin("ry", cut_copy(l, g), s != l)
 
     @scoped("reduce_done")
     def reduce_done(l, g):
-        copies = [
-            remote(
-                p1.at[l, 0, :, cols(g)], r2.at[l, k, :, cols(g)],
-                ry_send.at[l, g, k], ry_recv.at[l, g, k], yp[k],
-            )
-            for k in (0, 1, 2)
-        ]
+        if direct(l, g):
+            copies = [
+                remote(
+                    p1.at[l, 0, :, wcols(g)], r2.at[l, k, :, wcols(g)],
+                    ry_send.at[l, g, k], ry_recv.at[l, g, k], yp[k],
+                )
+                for k in (0, 1, 2)
+            ]
+        else:
+            copies = [pair_copy(l, g), cut_copy(l, g)]
 
         @pl.when(s == l)
         def _():
             for copy in copies:
                 copy.wait_recv()
-            total = p1[l, yl, :, cols(g)].astype(F32)
-            for k in (0, 1, 2):
-                total += r2[l, k, :, cols(g)].astype(F32)
-            wgrad_ref[:, cols(g)] = total
+            total = p1[l, yl, :, wcols(g)].astype(F32)
+            for k in range(len(copies)):
+                total += r2[l, k, :, wcols(g)].astype(F32)
+            wgrad_ref[:, wcols(g)] = total
 
     def spread_start(event, buf, h):
         mine = buf.at[t, part(h)]
@@ -325,25 +435,31 @@
         for _ in range(min(count, len(fills))):
             fills.pop(0)()
 
-    def weight_grad(lhs_ref, rhs_ref, c0, n, then=None):
+    def weight_grad(l, parts, lhs_ref, rhs_ref):
+        c0, n = REDUCE[parts[0]][0], sum(REDUCE[g][1] for g in parts)
+
         @scoped("weight_grad")
-        def one(i):
-            left = lhs_ref[:, :, i * 256:(i + 1) * 256].reshape(SEQ, 256).T
-            gt_s[...] = left
+        def one(step):
+            at = (x + step) % 4
+            gt_s[...] = lhs_ref[:, :, aligned(at, 256)].reshape(SEQ, 256).T
 
             def tile(j, _):
                 value = dot_nn(gt_s[...], rhs_ref[:, :, aligned(j, 256)].reshape(SEQ, 256))
-                gd[i, :, :, :, pl.ds(pl.multiple_of(c0 + j * 256, 256), 256)] = value.astype(
+                gd[at, :, :, :, pl.ds(pl.multiple_of(c0 + j * 256, 256), 256)] = value.astype(
                     BF16
                 ).reshape(2, 2, ROWS, 256)
                 return 0
 
             lax.fori_loop(0, n // 256, tile, 0)
-            if then is not None and i == 3:
-                then()
-
-        for i in range(4):
-            fills.append(functools.partial(one, i))
+            for g in parts:
+                begin(("rc", l, g), c_copy(l, g, step))
+
+        for step in (2, 1, 3, 0):
+            fills.append(functools.partial(one, step))
+
+    def reduce_all(l, g):
+        for step in (2, 1, 3, 0):
+            reduce_c(l, g, step)
 
     def cross_send(index, value, l, local_ref, h):
         @pl.when(s == l)
@@ -469,7 +585,9 @@
             if h == 0:
                 gather_done(l, 0)
             project(l, h)
+        gather_c(l, 1)
         attend(l)
+        gather_done(l, 1)
         for h in BOTH:
             share(4 * l + 1, h, lambda h=h: mixed_s[l, :, rows(h)], l, 768, 256)
 
@@ -557,13 +675,14 @@
     for k in range(4):
         pb[s, FC + k:FC + k + 1] = fc_ref[:, k * 1024:(k + 1) * 1024]
     pb[s, FC + 4:] = jnp.zeros((SMALL - FC - 4, D), F32)
-    begin("pb", remote(pb.at[s], pb.at[s], o_send.at[2, 0], o_recv.at[2, 0], across))
     for j in range(3):
         w[s, x, yl, c, :, j * 256:(j + 1) * 256] = qkv_ref[j]
+    gather_y(0)
     w[s, x, yl, c, :, 768:1024] = wo_ref[...]
-    gather_y(0)
+    gather_y(1)
     w[s, x, yl, c, :, 2048:] = fc2_ref[...]
-    turn_x(2)
+    turn_x(5)
+    begin("pb", remote(pb.at[s], pb.at[s], o_send.at[4, 0], o_recv.at[4, 0], across))
     w[s, x, yl, c, :, 1024:2048] = fc1_ref[...]
     late[...] = jnp.zeros_like(late)
     early[...] = jnp.zeros_like(early)
@@ -572,57 +691,73 @@
     places_i = lax.broadcasted_iota(jnp.int32, (SEQ, SEQ), 0)
     places_j = lax.broadcasted_iota(jnp.int32, (SEQ, SEQ), 1)
     mask_s[...] = jnp.where((seg_rows == seg_cols) & (places_i >= places_j), 1.0, 0.0)
+    gather_x(0, 0)
+    gather_y(2)
+    gather_x(0, 1)
+    gather_y(3)
+    gather_y(4)
+    turn_y(5)
     with jax.named_scope("wait_pb"):
-        remote(pb.at[1 - s], pb.at[1 - s], o_send.at[2, 0], o_recv.at[2, 0], across).wait_recv()
+        remote(pb.at[1 - s], pb.at[1 - s], o_send.at[4, 0], o_recv.at[4, 0], across).wait_recv()
     for h in BOTH:
         norm_one(0, h, x_ref[s, rows(h)].astype(F32))
-    gather_x(0, 0)
-    gather_y(1)
-    turn_y(2)
     gm[1, t] = cot_ref[s]
     for h in BOTH:
         spread_start(8, gm.at[1], h)
     dy_s[...] = cot_ref[s].astype(F32)
     early[1, 3:4] = row_sum(dy_s[...])
     gather_c(0, 0)
-    gather_x(0, 1)
+    for g in (2, 3, 4):
+        gather_x(0, g)
 
     attention_part(0)
+    gather_c(0, 2)
+    gather_x(1, 0)
+    gather_x(1, 1)
     for h in BOTH:
         norm_two(0, h)
-    gather_c(0, 1)
-    gather_x(1, 0)
+    gather_c(0, 3)
+    gather_c(0, 4)
+    turn_c(0, 5)
     for h in BOTH:
         spread_done(2, g2.at[0], h)
         if h == 0:
-            gather_done(0, 1)
+            gather_done(0, 2)
+            gather_done(0, 3)
         up(0, h)
         if h == 0:
-            turn_c(0, 2)
-            gather_done(0, 2)
+            gather_done(0, 4)
+            gather_done(0, 5)
         share(3, h, lambda h=h: active_s[0, :, rows(h)], 0, 2048, 1024)
-    turn_c(1, 2)
-    gather_c(1, 0)
-    gather_x(1, 1)
+    gather_x(1, 4)
+    gather_x(1, 2)
     for h in BOTH:
         hidden = layer_out(0, h)
         norm_one(1, h, hidden.astype(BF16).astype(F32))
         cross_send(0, hidden, 0, out_ref, h)
+        if h == 0:
+            gather_c(1, 0)
+    gather_x(1, 3)
+    turn_c(1, 5)
 
     attention_part(1)
-    gather_done(1, 2)
     for h in BOTH:
         spread_done(8, gm.at[1], h)
+    gather_c(1, 4)
+    gather_done(1, 5)
+    gather_c(1, 2)
+    gather_done(1, 4)
     before_up(1)
     for h in BOTH:
         norm_two(1, h)
-    gather_c(1, 1)
-    weight_grad(gm.at[1], active_s.at[1], 2048, 1024, lambda: reduce_c(1, 2))
-    weight_grad(g2.at[1], gb_s, 1024, 1024, lambda: reduce_c(1, 1))
+    gather_c(1, 3)
+    weight_grad(1, (3, 4), gm.at[1], active_s.at[1])
+    weight_grad(1, (2,), g2.at[1], gb_s)
     for h in BOTH:
         spread_done(6, g2.at[1], h)
         if h == 0:
-            gather_done(1, 1)
+            gather_done(1, 2)
+            gather_done(1, 3)
         up(1, h)
         share(9, h, lambda h=h: gb_s[:, rows(h)], 1, 1024, 1024)
     fill(4)
@@ -630,7 +765,8 @@
     fill(2)
     norm_two_back(1, 1)
     fill(1)
-    reduce_x(1, 2)
+    reduce_all(1, 3)
+    reduce_all(1, 4)
     fill(1)
     share(7, 0, lambda: active_s[1, :, rows(0)], 1, 2048, 1024)
     spread_done(10, ga.at[1], 0)
@@ -638,13 +774,14 @@
     share(7, 1, lambda: active_s[1, :, rows(1)], 1, 2048, 1024)
     spread_done(10, ga.at[1], 1)
     mixed_back(1, 1)
-    reduce_x(1, 1)
     attend_back(1)
     for h in BOTH:
         share(11, h, lambda h=h: gp_s[:, rows(h)], 1, 0, 768)
-    reduce_f(1, 2)
-    weight_grad(ga.at[1], mixed_s.at[1], 768, 256)
-    weight_grad(g1.at[1], gp_s, 0, 768, lambda: reduce_c(1, 0))
+    reduce_all(1, 2)
+    reduce_f(1, 3)
+    reduce_f(1, 4)
+    weight_grad(1, (0,), g1.at[1], gp_s)
+    weight_grad(1, (1,), ga.at[1], mixed_s.at[1])
     fill(8)
 
     def pass_grad(h):
@@ -655,76 +792,97 @@
         cross_send(3, grad.astype(F32), 1, grad_ref, h)
 
     pass_grad(0)
-    reduce_f(1, 1)
     for h in BOTH:
         hidden = layer_out(1, h)
         cross_send(2, hidden, 1, out_ref, h)
     pass_grad(1)
-    reduce_x(1, 0)
-    reduce_y(1, 2)
+    reduce_f(1, 2)
+    reduce_all(1, 0)
     early[0, 3:4] = row_sum(dy_s[...])
     for kind in BOTH:
         all_start(kind, 1, "c")
-    flush(("rc", 1, 2))
-    flush(("rx", 1, 2))
 
     for h in BOTH:
         spread_done(12, gm.at[0], h)
         down(0, h)
         share(13, h, lambda h=h: gb_s[:, rows(h)], 0, 1024, 1024)
+    for kind in BOTH:
+        all_next(kind, 1, "c", "y")
+    reduce_all(1, 1)
+    reduce_y(1, 3)
+    reduce_y(1, 4)
+    for g in (4, 3, 2):
+        flush(("rc", 1, g))
+        flush(("rx", 1, g))
+    weight_grad(0, (3, 4), gm.at[0], active_s.at[0])
+    weight_grad(0, (2,), g2.at[0], gb_s)
+    fill(4)
     reduce_f(1, 0)
-    weight_grad(gm.at[0], active_s.at[0], 2048, 1024, lambda: reduce_c(0, 2))
-    weight_grad(g2.at[0], gb_s, 1024, 1024, lambda: reduce_c(0, 1))
-    fill(4)
     norm_two_back(0, 0)
-    reduce_y(1, 1)
-    flush(("rc", 1, 1))
-    flush(("rx", 1, 1))
+    reduce_y(1, 2)
     fill(2)
     norm_two_back(0, 1)
-    reduce_x(0, 2)
+    reduce_f(1, 1)
+    reduce_all(0, 4)
+    reduce_all(0, 3)
     fill(2)
-    for kind in BOTH:
-        all_next(kind, 1, "c", "y")
+    reduce_g(1, 3)
+    reduce_g(1, 4)
     spread_done(14, ga.at[0], 0)
     mixed_back(0, 0)
+    reduce_g(1, 2)
     reduce_y(1, 0)
-    flush(("rc", 1, 0))
-    flush(("rx", 1, 0))
+    for kind in BOTH:
+        all_next(kind, 1, "y", "x")
     spread_done(14, ga.at[0], 1)
     mixed_back(0, 1)
-    reduce_x(0, 1)
+    reduce_all(0, 2)
     attend_back(0)
     for h in BOTH:
         share(15, h, lambda h=h: gp_s[:, rows(h)], 0, 0, 768)
+    all_start(1, 0, "c")
+    reduce_y(1, 1)
+    for g in (1, 0):
+        flush(("rc", 1, g))
+        flush(("rx", 1, g))
+    weight_grad(0, (1,), ga.at[0], mixed_s.at[0])
+    fill(4)
+    wide_y(0, 4)
+    reduce_f(0, 3)
+    reduce_g(1, 0)
+    weight_grad(0, (0,), g1.at[0], gp_s)
+    fill(3)
+    reduce_all(0, 1)
+    fill(1)
+    all_next(1, 0, "c", "y")
+    reduce_c(0, 0, 2)
     reduce_f(0, 2)
-    all_start(1, 0, "c")
-    weight_grad(ga.at[0], mixed_s.at[0], 768, 256)
-    weight_grad(g1.at[0], gp_s, 0, 768, lambda: reduce_c(0, 0))
-    fill(8)
+    for step in (1, 3, 0):
+        reduce_c(0, 0, step)
+    reduce_g(1, 1)
     cross_send(1, norm_one_back(0, 0), 0, grad_ref, 0)
-    reduce_f(0, 1)
-    all_next(1, 0, "c", "y")
     for kind in BOTH:
-        all_next(kind, 1, "y", "x")
+        all_next(kind, 1, "x", "z")
     cross_send(1, norm_one_back(0, 1), 0, grad_ref, 1)
     all_start(0, 0, "c")
-    reduce_x(0, 0)
     all_next(0, 0, "c", "z")
+    reduce_y(0, 3)
+    all_next(0, 0, "z", "y")
+    reduce_f(0, 1)
+    reduce_f(0, 0)
     reduce_y(0, 2)
-    for kind in BOTH:
-        all_next(kind, 1, "x", "z")
     all_next(1, 0, "y", "x")
+    wide_x(0, 4)
+    reduce_g(0, 3)
+    all_next(0, 0, "y", "x")
     reduce_y(0, 1)
-    all_next(0, 0, "z", "y")
-    reduce_f(0, 0)
-    all_next(0, 0, "y", "x")
+    reduce_y(0, 0)
     all_next(1, 0, "x", "z")
-    for g in (2, 1, 0):
+    reduce_g(0, 2)
+    for g in (4, 3, 2, 1, 0):
         reduce_done(1, g)
     for kind in BOTH:
         all_wait(kind, 1, "z")
-    reduce_y(0, 0)
     all_wait(0, 0, "x")
     all_wait(1, 0, "z")
     for kind, ref in ((0, late_ref), (1, early_ref)):
@@ -748,7 +906,8 @@
         def _():
             ref[1 - s] = xr[pairs[1]]
 
-    for g in (2, 1, 0):
+    wide_done(0, 4)
+    for g in (3, 2, 1, 0):
         reduce_done(0, g)
     for key in list(pending):
         flush(key)
@@ -787,6 +946,7 @@
         pltpu.VMEM((2, 4, 2, ROWS, WIDE), BF16),
         pltpu.VMEM((2, 6, ROWS, WIDE), BF16),
         pltpu.VMEM((2, 3, ROWS, WIDE), BF16),
+        pltpu.VMEM((2, 4, ROWS, 512), BF16),
         pltpu.VMEM((2, 2, ROWS, WIDE), BF16),
         pltpu.VMEM((2, SMALL, D), F32),
         pltpu.VMEM((2, 4, ROWS, D), BF16),
@@ -818,13 +978,13 @@
         scratch += [pltpu.VMEM((2, n, 8, width), F32) for n in (2, 4, 4, 4)]
     scratch += [
         dma((16, 2, 3)), dma((16, 2, 3)),
-        dma((3, 3)), dma((2, 3, 3)),
-        dma((2, 3, 3)), dma((2, 3, 3)),
-        dma((2, 3)), dma((2, 3)),
-        dma((2, 3)), dma((2, 3)),
-        dma((2, 3, 6)), dma((2, 3, 6)),
-        dma((2, 3, 3)), dma((2, 3, 3)),
-        dma((4, 2)), dma((4, 2)),
+        dma((6, 3)), dma((2, 6, 3)),
+        dma((2, 6, 3)), dma((2, 6, 3)),
+        dma((2, 6)), dma((2, 6)),
+        dma((2, 5, 4)), dma((2, 5, 4)),
+        dma((2, 5, 6)), dma((2, 5, 6)),
+        dma((2, 5, 3)), dma((2, 5, 3)),
+        dma((5, 2)), dma((5, 2)),
         dma((2, 2, 10)), dma((2, 2, 10)),
     ]
     sums = pl.pallas_call(

time: 176 us -> 168 us (0.955)
  Pallas kernels: 175 us -> 166 us
    pallas_call x1, Pallas kernels: 172 us -> 163 us  [fused(): pl.pallas_call(kernel, out_shape=(jax.ShapeDtypeStruct((2, ROWS, D), F32)...]
where the time goes in v3:
time: 168 us; the launch traced here: 167 us
  Pallas kernels  166 us (99%)
    pallas_call x1, Pallas kernels, fused(): pl.pallas_call(kernel, out_shape=(jax.ShapeDtypeStruct((2, ROWS, D), F32)...  163 us

profile of v3, /device:TPU:0, one launch (start us, length us, event | category | flops | bytes accessed | tf_op | source)
XLA Modules:
  0.0 166.7 jit_solution(16261481277270399407)
XLA Ops:
  0.6 163.2 %shard_map.203 = (f32[2,64,1024]{2,1,0:T(8,128)}, f32[2,64,1024]{2,1,0:T(8,128)}, f32[64,3072]{1,0:T(8,128)}, f32[8,512]{1,0:T(8,128)}, f32[8,1024]{1,0:T(8,128)}) custom-call(bf16[2,64,1024]{2,1,0:T(8,128)(2,1)} %x_ref.1, bf16[2,64,1024]{2,1,0:T(8,128)(2,1)} %cot_ref.1, s32[2,1,256]{2,1,0:T(1,128)} %seg_ref.1, bf16[3,64,256]{2,1,0:T(8,128)(2,1)} %bitcast.19, ...), custom_call_target="tpu_custom_call" | custom-call | tf_op jit(solution)/shard_map/pallas_call | solution.py:990
  163.8 2.7 %shard_map.204 = (f32[1,2,64,1024]{3,2,1,0:T(8,128)}, f32[1,2,64,1024]{3,2,1,0:T(8,128)}, f32[1,3,64,256]{3,2,1,0:T(8,128)}, f32[1,64,256]{2,1,0:T(8,128)}, f32[...) custom-call(f32[2,64,1024]{2,1,0:T(8,128)} %get-tuple-element.27.out, ...), custom_call_target="tpu_custom_call" | custom-call | tf_op jit(solution)/shard_map/pallas_call | solution.py:1006

commit v4 on v3

--- a/solution.py
+++ b/solution.py
@@ -468,7 +468,7 @@
 
         @pl.when(s != l)
         def _():
-            xs[index, rows(h)] = value
+            xs[index, rows(h)] = value.astype(BF16)
 
         begin("o", remote(
             xs.at[index, part(h)], xr.at[index, part(h)], o_send.at[index, h], o_recv.at[index, h], across
@@ -822,6 +822,7 @@
     reduce_y(1, 2)
     fill(2)
     norm_two_back(0, 1)
+    all_start(1, 0, "c")
     reduce_f(1, 1)
     reduce_all(0, 4)
     reduce_all(0, 3)
@@ -837,10 +838,10 @@
     spread_done(14, ga.at[0], 1)
     mixed_back(0, 1)
     reduce_all(0, 2)
+    all_next(1, 0, "c", "y")
     attend_back(0)
     for h in BOTH:
         share(15, h, lambda h=h: gp_s[:, rows(h)], 0, 0, 768)
-    all_start(1, 0, "c")
     reduce_y(1, 1)
     for g in (1, 0):
         flush(("rc", 1, g))
@@ -854,7 +855,7 @@
     fill(3)
     reduce_all(0, 1)
     fill(1)
-    all_next(1, 0, "c", "y")
+    all_next(1, 0, "y", "x")
     reduce_c(0, 0, 2)
     reduce_f(0, 2)
     for step in (1, 3, 0):
@@ -868,16 +869,15 @@
     all_next(0, 0, "c", "z")
     reduce_y(0, 3)
     all_next(0, 0, "z", "y")
+    reduce_f(0, 0)
     reduce_f(0, 1)
-    reduce_f(0, 0)
+    all_next(1, 0, "x", "z")
     reduce_y(0, 2)
-    all_next(1, 0, "y", "x")
+    all_next(0, 0, "y", "x")
     wide_x(0, 4)
     reduce_g(0, 3)
-    all_next(0, 0, "y", "x")
+    reduce_y(0, 0)
     reduce_y(0, 1)
-    reduce_y(0, 0)
-    all_next(1, 0, "x", "z")
     reduce_g(0, 2)
     for g in (4, 3, 2, 1, 0):
         reduce_done(1, g)
@@ -900,11 +900,11 @@
 
         @pl.when(s == 0)
         def _():
-            ref[1 - s] = xr[pairs[0]]
+            ref[1 - s] = xr[pairs[0]].astype(F32)
 
         @pl.when(s == 1)
         def _():
-            ref[1 - s] = xr[pairs[1]]
+            ref[1 - s] = xr[pairs[1]].astype(F32)
 
     wide_done(0, 4)
     for g in (3, 2, 1, 0):
@@ -969,8 +969,8 @@
         pltpu.VMEM((256, SEQ), BF16),
         pltpu.VMEM((SEQ, SEQ), F32),
         pltpu.VMEM((ROWS, D), F32),
-        pltpu.VMEM((4, ROWS, D), F32),
-        pltpu.VMEM((4, ROWS, D), F32),
+        pltpu.VMEM((4, ROWS, D), BF16),
+        pltpu.VMEM((4, ROWS, D), BF16),
         pltpu.VMEM((2, 8, 512), F32),
         pltpu.VMEM((2, 8, D), F32),
     ]

time: 168 us -> 168 us (level)
  no operation moved by 1% of the time
where the time goes in v4:
time: 168 us; the launch traced here: 167 us
  Pallas kernels  166 us (99%)
    pallas_call x1, Pallas kernels, fused(): pl.pallas_call(kernel, out_shape=(jax.ShapeDtypeStruct((2, ROWS, D), F32)...  164 us

profile of v4, /device:TPU:0, one launch (start us, length us, event | category | flops | bytes accessed | tf_op | source)
XLA Modules:
  0.0 167.1 jit_solution(13403928454537387320)
XLA Ops:
  0.6 163.6 %shard_map.203 = (f32[2,64,1024]{2,1,0:T(8,128)}, f32[2,64,1024]{2,1,0:T(8,128)}, f32[64,3072]{1,0:T(8,128)}, f32[8,512]{1,0:T(8,128)}, f32[8,1024]{1,0:T(8,128)}) custom-call(bf16[2,64,1024]{2,1,0:T(8,128)(2,1)} %x_ref.1, bf16[2,64,1024]{2,1,0:T(8,128)(2,1)} %cot_ref.1, s32[2,1,256]{2,1,0:T(1,128)} %seg_ref.1, bf16[3,64,256]{2,1,0:T(8,128)(2,1)} %bitcast.19, ...), custom_call_target="tpu_custom_call" | custom-call | tf_op jit(solution)/shard_map/pallas_call | solution.py:990
  164.3 2.7 %shard_map.204 = (f32[1,2,64,1024]{3,2,1,0:T(8,128)}, f32[1,2,64,1024]{3,2,1,0:T(8,128)}, f32[1,3,64,256]{3,2,1,0:T(8,128)}, f32[1,64,256]{2,1,0:T(8,128)}, f32[...) custom-call(f32[2,64,1024]{2,1,0:T(8,128)} %get-tuple-element.27.out, ...), custom_call_target="tpu_custom_call" | custom-call | tf_op jit(solution)/shard_map/pallas_call | solution.py:1006
